TPU v7x, 128 devices: a whole 4x4x4 slice. The times are simulated.
128 devices in a mesh: exp: 8 (over z, core), pix: 16 (over x, y).
Axes of the slice: x: 4, y: 4, z: 4, core: 2. Of those that a mesh axis runs over, the one named last changes fastest.
Arguments:
- sky: bfloat16 [512, 512, 512], P('exp', 'pix'), may hold values from -6 to 6
- kernels: bfloat16 [6, 25, 25], replicated, may hold values from -0.25 to 0.25
- coefs: bfloat16 [32, 6, 512, 1536], P('exp', None, 'pix'), may hold values from 0.19921875 to 1
- observed: float32 [32, 512, 1536], P('exp', 'pix'), may hold values from -8 to 8
- inv_var: bfloat16 [32, 512, 1536], P('exp', 'pix'), may hold values from 0.25 to 4
- footprints: int32 [32, 8], replicated, may hold values from 0 to 511, as said below
- offsets: int32 [32, 2], replicated, may hold values from 0 to 500, as said below
- tile_slot: int32 [512], replicated, may hold values from 0 to 511, as said below
Outputs:
- sky_gradient: float32 [512, 512, 512], P('exp', 'pix')
Inputs may be any that keep to these rules, and one draw needn't show every extreme that they name: `footprints`: exposure e reads tile row r and the row below it, columns c to c + 3 of the sky grid of 32 x 16 tiles (tile id = 16 row + column): entry 4 i + j is tile (r + i, c + j). Exposures are dealt to exp in blocks of 4. Column 0 is a row offset, a multiple of 32 below 512; the row offsets of the 4 exposures of one block differ from one another after division by 32. Column 1 is a column offset from 12 to 500. `tile_slot`: A permutation. The four tiles of one tile row of any footprint lie in four different blocks of 64 storage rows.
All inputs are finite; a program needn't handle non-finite values.
Results may differ from a plain program's by a relative error of at most 0.01.
Values may be sent and summed in bfloat16 or wider, within the bound.
A program may use at most 128 MiB of HBM per device.

v0:
```python
import jax
import jax.numpy as jnp
from jax import lax
from jax.sharding import PartitionSpec as P


def with_halo(block, sides, width):
    for axis, dim in sides:
        count = lax.axis_size(axis)
        forward = [(i, i + 1) for i in range(count - 1)]
        backward = [(target, source) for source, target in forward]
        low = lax.ppermute(
            lax.slice_in_dim(block, block.shape[dim] - width, None, axis=dim), axis, forward
        )
        high = lax.ppermute(lax.slice_in_dim(block, 0, width, axis=dim), axis, backward)
        block = jnp.concatenate([low, block, high], axis=dim)
    return block


def passed_along(x, axis, by):
    peers = lax.axis_size(axis)
    pairs = [(i, i + by) for i in range(peers) if 0 <= i + by < peers]
    return lax.ppermute(x, axis, pairs)


def owned_rows(tiles, owner_of, local_of, group_index):
    belongs = owner_of[tiles] == group_index
    which = jnp.argmax(belongs.astype(jnp.int32), axis=-1)
    chosen = jnp.take_along_axis(tiles, which[..., None], axis=-1)[..., 0]
    return (local_of[chosen], jnp.any(belongs, axis=-1))


def local(sky, kernels, coefs, observed, inv_var, footprints, offsets, tile_slot):
    group_count = lax.axis_size("exp")
    strip_count = lax.axis_size("pix")
    group_index = lax.axis_index("exp")
    strip_index = lax.axis_index("pix")
    stored, strip_rows, tile_side = sky.shape
    visits = observed.shape[0]
    image_width = observed.shape[2]
    kernel_side = kernels.shape[1]
    basis_count = kernels.shape[0]
    margin = kernel_side // 2
    owner_of = tile_slot // stored
    local_of = tile_slot % stored
    blocks = footprints.reshape(group_count, visits, 2, 4)
    phases = (offsets[:, 0] // strip_rows).reshape(group_count, visits)
    shifts = offsets[:, 1].reshape(group_count, visits)
    my_phase = phases[group_index]
    my_shift = shifts[group_index]
    visit_range = jnp.arange(visits)
    strip_range = jnp.arange(strip_count)
    nothing = jnp.zeros((), sky.dtype)
    lower_row = strip_index < phases
    row_tiles = jnp.where(lower_row[..., None], blocks[:, :, 1], blocks[:, :, 0])
    held_rows, held = owned_rows(row_tiles, owner_of, local_of, group_index)
    outgoing = jnp.where(held[..., None, None], sky[held_rows], nothing)
    arrived = lax.all_to_all(outgoing, "exp", split_axis=0, concat_axis=0, tiled=True)
    source = owner_of[row_tiles[group_index]]
    picked = arrived[source, visit_range[:, None]]
    matching = (my_phase[None, :] + strip_range[:, None]) % strip_count == strip_index
    chosen = jnp.argmax(matching.astype(jnp.int32), axis=1)
    present = jnp.any(matching, axis=1)
    forward_rows = jnp.where(present[:, None, None, None], picked[chosen], nothing)
    landed = lax.all_to_all(forward_rows, "pix", split_axis=0, concat_axis=0, tiled=True)
    mine = landed[(my_phase + strip_index) % strip_count]
    band = mine.transpose(0, 2, 1, 3).reshape(visits, strip_rows, 4 * tile_side)
    padded = with_halo(band, (("pix", 1),), margin)

    def cut_window(image, start):
        return lax.dynamic_slice_in_dim(image, start - margin, image_width + 2 * margin, 1)

    windows = jax.vmap(cut_window)(padded, my_shift)
    block_cols = tile_side // 4
    block_count = image_width // block_cols
    patch_cols = block_cols + 2 * margin
    padded_rows = strip_rows + 2 * margin
    kernel_range = jnp.arange(kernel_side)
    patch_range = jnp.arange(patch_cols)
    column_range = jnp.arange(block_cols)
    hot_table = (
        patch_range[None, :, None] - column_range[None, None, :] == kernel_range[:, None, None]
    ).astype(jnp.float32)
    band_table = jnp.einsum("buv,vcj->ucbj", kernels.astype(jnp.float32), hot_table).astype(
        jnp.bfloat16
    )
    band_table = band_table.reshape(kernel_side, patch_cols, basis_count * block_cols)
    main_part = windows[:, :, :image_width].reshape(visits, padded_rows, block_count, block_cols)
    tail_source = jnp.pad(
        windows[:, :, block_cols:], ((0, 0), (0, 0), (0, block_cols - 2 * margin))
    )
    tail_part = tail_source.reshape(visits, padded_rows, block_count, block_cols)[..., : 2 * margin]
    patches = jnp.concatenate([main_part, tail_part], axis=3)

    def forward_step(kernel_row, running):
        rows = lax.dynamic_slice_in_dim(patches, kernel_row, strip_rows, 1)
        table = lax.dynamic_index_in_dim(band_table, kernel_row, 0, keepdims=False)
        return running + jnp.einsum(
            "eykc,cn->eykn", rows, table, preferred_element_type=jnp.float32
        )

    running = jnp.zeros((visits, strip_rows, block_count, basis_count * block_cols), jnp.float32)
    running = lax.fori_loop(0, kernel_side, forward_step, running)
    blurred = (
        running.reshape(visits, strip_rows, block_count, basis_count, block_cols)
        .transpose(0, 3, 1, 2, 4)
        .reshape(visits, basis_count, strip_rows, image_width)
    )
    coef_wide = coefs.astype(jnp.float32)
    model = jnp.sum(coef_wide * blurred, axis=1)
    resid = inv_var.astype(jnp.float32) * (model - observed)
    weighted = (coef_wide * resid[:, None]).astype(jnp.bfloat16)
    spread = (
        weighted.reshape(visits, basis_count, strip_rows, block_count, block_cols)
        .transpose(0, 2, 3, 1, 4)
        .reshape(visits, strip_rows, block_count, basis_count * block_cols)
    )

    def adjoint_step(kernel_row, growing):
        table = lax.dynamic_index_in_dim(band_table, kernel_row, 0, keepdims=False)
        term = jnp.einsum("eykn,cn->eykc", spread, table, preferred_element_type=jnp.float32)
        current = lax.dynamic_slice_in_dim(growing, kernel_row, strip_rows, 1)
        return lax.dynamic_update_slice_in_dim(growing, current + term, kernel_row, 1)

    growing = jnp.zeros((visits, padded_rows, block_count, patch_cols), jnp.float32)
    growing = lax.fori_loop(0, kernel_side, adjoint_step, growing)
    main_back = growing[..., :block_cols].reshape(visits, padded_rows, image_width)
    tail_back = jnp.pad(
        growing[..., block_cols:], ((0, 0), (0, 0), (0, 0), (0, block_cols - 2 * margin))
    ).reshape(visits, padded_rows, image_width)
    back = (
        jnp.pad(main_back, ((0, 0), (0, 0), (0, 2 * margin)))
        + jnp.pad(tail_back, ((0, 0), (0, 0), (block_cols, 0)))[:, :, : image_width + 2 * margin]
    )
    from_lower = passed_along(back[:, strip_rows + margin :].astype(jnp.bfloat16), "pix", 1).astype(
        jnp.float32
    )
    from_upper = passed_along(back[:, :margin].astype(jnp.bfloat16), "pix", -1).astype(jnp.float32)
    center = back[:, margin : margin + strip_rows]
    center = center.at[:, :margin].add(from_lower)
    center = center.at[:, strip_rows - margin :].add(from_upper)

    def place_piece(piece, start):
        canvas = jnp.zeros((strip_rows, 4 * tile_side), jnp.float32)
        return lax.dynamic_update_slice_in_dim(canvas, piece, start - margin, 1)

    placed = jax.vmap(place_piece)(center, my_shift)
    pieces = (
        placed.reshape(visits, strip_rows, 4, tile_side).transpose(0, 2, 1, 3).astype(jnp.bfloat16)
    )
    gradient = jnp.zeros((stored, strip_rows, tile_side), jnp.float32)
    back_match = (my_phase[None, :] + strip_index) % strip_count == strip_range[:, None]
    back_visit = jnp.argmax(back_match.astype(jnp.int32), axis=1)
    back_has = jnp.any(back_match, axis=1)
    to_rows = jnp.where(back_has[:, None, None, None], pieces[back_visit], nothing)
    gathered = lax.all_to_all(to_rows, "pix", split_axis=0, concat_axis=0, tiled=True)
    per_visit = gathered[(strip_index - my_phase) % strip_count]
    owners_row = owner_of[row_tiles[group_index]]
    selector = (owners_row[None] == jnp.arange(group_count)[:, None, None]).astype(jnp.bfloat16)
    to_owners = jnp.einsum(
        "gqj,qjst->gqst", selector, per_visit, preferred_element_type=jnp.float32
    ).astype(jnp.bfloat16)
    returned = lax.all_to_all(to_owners, "exp", split_axis=0, concat_axis=0, tiled=True)
    terms = jnp.where(held[..., None, None], returned.astype(jnp.float32), 0.0)
    gradient = gradient.at[held_rows.reshape(-1)].add(terms.reshape(-1, strip_rows, tile_side))
    return gradient


def solution(mesh):
    return jax.shard_map(
        local,
        mesh=mesh,
        in_specs=(
            P("exp", "pix", None),
            P(),
            P("exp", None, "pix", None),
            P("exp", "pix", None),
            P("exp", "pix", None),
            P(),
            P(),
            P(),
        ),
        out_specs=P("exp", "pix", None),
        check_vma=False,
    )
```

profile of v0, /device:TPU:1, one launch (start us, length us, event | category | flops | bytes accessed | tf_op | source)
XLA Modules:
  0.0 732.4 jit_solution(13447818532843554735)
XLA Ops:
  9.6 6.8 all-to-all-start
  18.5 13.0 %all-to-all-done = bf16[8,4,32,512]{3,2,1,0:T(8,128)(2,1)S(1)} async-done(((bf16[8,4,32,512]{3,2,1,0:T(8,128)(2,1)}), bf16[8,4,32,512]{3,2,1,0:T(8,128)(2,1)S(1)}, u32[]{:S(2)}, u32[]{:S(2)}) %all-to-all-start) | async-done | bytes 1048608 | tf_op jit(solution)/shard_map/all_to_all | solution.py:58
  37.3 6.9 all-to-all-start.1
  46.5 5.6 copy.137
  52.1 13.1 %reshape.424 = bf16[25,152,768]{2,1,0:T(8,128)(2,1)} reshape(bf16[25,152,6,128]{3,2,1,0:T(8,128)(2,1)} %copy.137) | data formatting | bytes 11673600 | tf_op jit(solution)/shard_map/reshape | solution.py:87
  81.1 8.0 %while.32 = (s32[]{:T(128)}, bf16[4,56,2048]{2,1,0:T(8,128)(2,1)S(1)}, s32[4,3]{1,0:T(4,128)S(1)}, bf16[4,56,1560]{2,1,0:T(8,128)(2,1)S(1)}, s32[]{:T(128)}) while((s32[]{:T(128)}, bf16[4,56,2048]{2,1,0:T(8,128)(2,1)S(1)}, s32[4,3]{1,0:T(4,128)S(1)}, bf16[4,56,1560]{2,1,0:T(8,128)(2,1)S(1)}, s32[]{:T(128)}) %tuple.138), condition=%wide.while_cond.2, body=%wide.while_body.2.sunk | while | flops 2 | bytes 372853 | solution.py:71
  91.1 134.6 %while.34 = (s32[]{:T(128)}, f32[4,32,12,768]{3,1,2,0:T(8,128)}, bf16[4,56,12,152]{3,1,2,0:T(8,128)(2,1)S(1)}, bf16[25,152,768]{2,1,0:T(8,128)(2,1)}, s32[]{:T(128)}, /*index=5*/s32[]{:T(128)}) while((s32[]{:T(128)}, f32[4,32,12,768]{3,1,2,0:T(8,128)}, bf16[4,56,12,152]{3,1,2,0:T(8,128)(2,1)S(1)}, bf16[25,152,768]{2,1,0:T(8,128)(2,1)}, ...), condition=%wide.region_6.7_spmd.clone, body=%wide.region_5.6_spmd.clone.sunk | while | flops 360972288 | bytes 10458191 | solution.py:103
  138.5 5.4 select_add_fusion.2
  182.1 5.5 select_add_fusion.2
  193.0 5.5 select_add_fusion.2
  203.9 5.5 select_add_fusion.2
  214.8 5.5 select_add_fusion.2
  225.7 6.6 reshape.428
  232.3 8.2 %copy.145 = f32[4,6,32,12,128]{4,3,2,1,0:T(8,128)} copy(f32[4,6,32,12,128]{4,1,2,3,0:T(8,128)} %bitcast.138) | data formatting | bytes 9437184 | tf_op jit(solution)/shard_map/transpose | solution.py:106
  240.5 6.7 reshape.429
  265.5 6.0 reshape.431
  273.2 334.1 %while.31 = (s32[]{:T(128)}, f32[4,56,12,152]{3,1,2,0:T(8,128)}, bf16[25,152,768]{2,1,0:T(8,128)(2,1)}, bf16[4,32,12,768]{3,1,2,0:T(8,128)(2,1)}, s32[]{:T(128)}, /*index=5*/s32[]{:T(128)}) while((s32[]{:T(128)}, f32[4,56,12,152]{3,1,2,0:T(8,128)}, bf16[25,152,768]{2,1,0:T(8,128)(2,1)}, bf16[4,32,12,768]{3,1,2,0:T(8,128)(2,1)}, s32[]{:T(128)}, ...), condition=%wide.region_9.10_spmd, body=%wide.region_8.9_spmd.sunk | while | flops 358846464 | bytes 6968393 | solution.py:126
  276.4 10.3 %dynamic_update_slice.8 = f32[4,56,12,152]{3,1,2,0:T(8,128)} dynamic-update-slice(f32[4,56,12,152]{3,1,2,0:T(8,128)} %get-tuple-element.502, f32[4,32,12,152]{3,1,2,0:T(8,128)S(1)} %bitcast_add_fusion.2, s32[]{:T(128)} %constant.241.clone.1..sunk, s32[]{:T(128)} %get-tuple-element.501, s32[]{:T(128)} %constant.241.clone.1..sunk, s32[]{:T(128)} %constant.241.clone.1..sunk) | dynamic-update-slice | bytes 1867780 | tf_op jit(solution)/shard_map/while/body/eval_jaxpr/dynamic_update_slice | solution.py:123
  290.0 10.3 %dynamic_update_slice.8 = f32[4,56,12,152]{3,1,2,0:T(8,128)} dynamic-update-slice(f32[4,56,12,152]{3,1,2,0:T(8,128)} %get-tuple-element.502, f32[4,32,12,152]{3,1,2,0:T(8,128)S(1)} %bitcast_add_fusion.2, s32[]{:T(128)} %constant.241.clone.1..sunk, s32[]{:T(128)} %get-tuple-element.501, s32[]{:T(128)} %constant.241.clone.1..sunk, s32[]{:T(128)} %constant.241.clone.1..sunk) | dynamic-update-slice | bytes 1867780 | tf_op jit(solution)/shard_map/while/body/eval_jaxpr/dynamic_update_slice | solution.py:123
  303.5 10.3 %dynamic_update_slice.8 = f32[4,56,12,152]{3,1,2,0:T(8,128)} dynamic-update-slice(f32[4,56,12,152]{3,1,2,0:T(8,128)} %get-tuple-element.502, f32[4,32,12,152]{3,1,2,0:T(8,128)S(1)} %bitcast_add_fusion.2, s32[]{:T(128)} %constant.241.clone.1..sunk, s32[]{:T(128)} %get-tuple-element.501, s32[]{:T(128)} %constant.241.clone.1..sunk, s32[]{:T(128)} %constant.241.clone.1..sunk) | dynamic-update-slice | bytes 1867780 | tf_op jit(solution)/shard_map/while/body/eval_jaxpr/dynamic_update_slice | solution.py:123
  317.0 10.3 %dynamic_update_slice.8 = f32[4,56,12,152]{3,1,2,0:T(8,128)} dynamic-update-slice(f32[4,56,12,152]{3,1,2,0:T(8,128)} %get-tuple-element.502, f32[4,32,12,152]{3,1,2,0:T(8,128)S(1)} %bitcast_add_fusion.2, s32[]{:T(128)} %constant.241.clone.1..sunk, s32[]{:T(128)} %get-tuple-element.501, s32[]{:T(128)} %constant.241.clone.1..sunk, s32[]{:T(128)} %constant.241.clone.1..sunk) | dynamic-update-slice | bytes 1867780 | tf_op jit(solution)/shard_map/while/body/eval_jaxpr/dynamic_update_slice | solution.py:123
  330.5 10.3 %dynamic_update_slice.8 = f32[4,56,12,152]{3,1,2,0:T(8,128)} dynamic-update-slice(f32[4,56,12,152]{3,1,2,0:T(8,128)} %get-tuple-element.502, f32[4,32,12,152]{3,1,2,0:T(8,128)S(1)} %bitcast_add_fusion.2, s32[]{:T(128)} %constant.241.clone.1..sunk, s32[]{:T(128)} %get-tuple-element.501, s32[]{:T(128)} %constant.241.clone.1..sunk, s32[]{:T(128)} %constant.241.clone.1..sunk) | dynamic-update-slice | bytes 1867780 | tf_op jit(solution)/shard_map/while/body/eval_jaxpr/dynamic_update_slice | solution.py:123
  344.0 10.3 %dynamic_update_slice.8 = f32[4,56,12,152]{3,1,2,0:T(8,128)} dynamic-update-slice(f32[4,56,12,152]{3,1,2,0:T(8,128)} %get-tuple-element.502, f32[4,32,12,152]{3,1,2,0:T(8,128)S(1)} %bitcast_add_fusion.2, s32[]{:T(128)} %constant.241.clone.1..sunk, s32[]{:T(128)} %get-tuple-element.501, s32[]{:T(128)} %constant.241.clone.1..sunk, s32[]{:T(128)} %constant.241.clone.1..sunk) | dynamic-update-slice | bytes 1867780 | tf_op jit(solution)/shard_map/while/body/eval_jaxpr/dynamic_update_slice | solution.py:123
  357.5 10.3 %dynamic_update_slice.8 = f32[4,56,12,152]{3,1,2,0:T(8,128)} dynamic-update-slice(f32[4,56,12,152]{3,1,2,0:T(8,128)} %get-tuple-element.502, f32[4,32,12,152]{3,1,2,0:T(8,128)S(1)} %bitcast_add_fusion.2, s32[]{:T(128)} %constant.241.clone.1..sunk, s32[]{:T(128)} %get-tuple-element.501, s32[]{:T(128)} %constant.241.clone.1..sunk, s32[]{:T(128)} %constant.241.clone.1..sunk) | dynamic-update-slice | bytes 1867780 | tf_op jit(solution)/shard_map/while/body/eval_jaxpr/dynamic_update_slice | solution.py:123
  371.1 10.3 %dynamic_update_slice.8 = f32[4,56,12,152]{3,1,2,0:T(8,128)} dynamic-update-slice(f32[4,56,12,152]{3,1,2,0:T(8,128)} %get-tuple-element.502, f32[4,32,12,152]{3,1,2,0:T(8,128)S(1)} %bitcast_add_fusion.2, s32[]{:T(128)} %constant.241.clone.1..sunk, s32[]{:T(128)} %get-tuple-element.501, s32[]{:T(128)} %constant.241.clone.1..sunk, s32[]{:T(128)} %constant.241.clone.1..sunk) | dynamic-update-slice | bytes 1867780 | tf_op jit(solution)/shard_map/while/body/eval_jaxpr/dynamic_update_slice | solution.py:123
  384.6 10.2 %dynamic_update_slice.8 = f32[4,56,12,152]{3,1,2,0:T(8,128)} dynamic-update-slice(f32[4,56,12,152]{3,1,2,0:T(8,128)} %get-tuple-element.502, f32[4,32,12,152]{3,1,2,0:T(8,128)S(1)} %bitcast_add_fusion.2, s32[]{:T(128)} %constant.241.clone.1..sunk, s32[]{:T(128)} %get-tuple-element.501, s32[]{:T(128)} %constant.241.clone.1..sunk, s32[]{:T(128)} %constant.241.clone.1..sunk) | dynamic-update-slice | bytes 1867780 | tf_op jit(solution)/shard_map/while/body/eval_jaxpr/dynamic_update_slice | solution.py:123
  398.0 10.2 %dynamic_update_slice.8 = f32[4,56,12,152]{3,1,2,0:T(8,128)} dynamic-update-slice(f32[4,56,12,152]{3,1,2,0:T(8,128)} %get-tuple-element.502, f32[4,32,12,152]{3,1,2,0:T(8,128)S(1)} %bitcast_add_fusion.2, s32[]{:T(128)} %constant.241.clone.1..sunk, s32[]{:T(128)} %get-tuple-element.501, s32[]{:T(128)} %constant.241.clone.1..sunk, s32[]{:T(128)} %constant.241.clone.1..sunk) | dynamic-update-slice | bytes 1867780 | tf_op jit(solution)/shard_map/while/body/eval_jaxpr/dynamic_update_slice | solution.py:123
  411.4 10.2 %dynamic_update_slice.8 = f32[4,56,12,152]{3,1,2,0:T(8,128)} dynamic-update-slice(f32[4,56,12,152]{3,1,2,0:T(8,128)} %get-tuple-element.502, f32[4,32,12,152]{3,1,2,0:T(8,128)S(1)} %bitcast_add_fusion.2, s32[]{:T(128)} %constant.241.clone.1..sunk, s32[]{:T(128)} %get-tuple-element.501, s32[]{:T(128)} %constant.241.clone.1..sunk, s32[]{:T(128)} %constant.241.clone.1..sunk) | dynamic-update-slice | bytes 1867780 | tf_op jit(solution)/shard_map/while/body/eval_jaxpr/dynamic_update_slice | solution.py:123
  424.8 10.2 %dynamic_update_slice.8 = f32[4,56,12,152]{3,1,2,0:T(8,128)} dynamic-update-slice(f32[4,56,12,152]{3,1,2,0:T(8,128)} %get-tuple-element.502, f32[4,32,12,152]{3,1,2,0:T(8,128)S(1)} %bitcast_add_fusion.2, s32[]{:T(128)} %constant.241.clone.1..sunk, s32[]{:T(128)} %get-tuple-element.501, s32[]{:T(128)} %constant.241.clone.1..sunk, s32[]{:T(128)} %constant.241.clone.1..sunk) | dynamic-update-slice | bytes 1867780 | tf_op jit(solution)/shard_map/while/body/eval_jaxpr/dynamic_update_slice | solution.py:123
  438.2 10.2 %dynamic_update_slice.8 = f32[4,56,12,152]{3,1,2,0:T(8,128)} dynamic-update-slice(f32[4,56,12,152]{3,1,2,0:T(8,128)} %get-tuple-element.502, f32[4,32,12,152]{3,1,2,0:T(8,128)S(1)} %bitcast_add_fusion.2, s32[]{:T(128)} %constant.241.clone.1..sunk, s32[]{:T(128)} %get-tuple-element.501, s32[]{:T(128)} %constant.241.clone.1..sunk, s32[]{:T(128)} %constant.241.clone.1..sunk) | dynamic-update-slice | bytes 1867780 | tf_op jit(solution)/shard_map/while/body/eval_jaxpr/dynamic_update_slice | solution.py:123
  451.6 10.2 %dynamic_update_slice.8 = f32[4,56,12,152]{3,1,2,0:T(8,128)} dynamic-update-slice(f32[4,56,12,152]{3,1,2,0:T(8,128)} %get-tuple-element.502, f32[4,32,12,152]{3,1,2,0:T(8,128)S(1)} %bitcast_add_fusion.2, s32[]{:T(128)} %constant.241.clone.1..sunk, s32[]{:T(128)} %get-tuple-element.501, s32[]{:T(128)} %constant.241.clone.1..sunk, s32[]{:T(128)} %constant.241.clone.1..sunk) | dynamic-update-slice | bytes 1867780 | tf_op jit(solution)/shard_map/while/body/eval_jaxpr/dynamic_update_slice | solution.py:123
  465.0 10.2 %dynamic_update_slice.8 = f32[4,56,12,152]{3,1,2,0:T(8,128)} dynamic-update-slice(f32[4,56,12,152]{3,1,2,0:T(8,128)} %get-tuple-element.502, f32[4,32,12,152]{3,1,2,0:T(8,128)S(1)} %bitcast_add_fusion.2, s32[]{:T(128)} %constant.241.clone.1..sunk, s32[]{:T(128)} %get-tuple-element.501, s32[]{:T(128)} %constant.241.clone.1..sunk, s32[]{:T(128)} %constant.241.clone.1..sunk) | dynamic-update-slice | bytes 1867780 | tf_op jit(solution)/shard_map/while/body/eval_jaxpr/dynamic_update_slice | solution.py:123
  478.4 10.2 %dynamic_update_slice.8 = f32[4,56,12,152]{3,1,2,0:T(8,128)} dynamic-update-slice(f32[4,56,12,152]{3,1,2,0:T(8,128)} %get-tuple-element.502, f32[4,32,12,152]{3,1,2,0:T(8,128)S(1)} %bitcast_add_fusion.2, s32[]{:T(128)} %constant.241.clone.1..sunk, s32[]{:T(128)} %get-tuple-element.501, s32[]{:T(128)} %constant.241.clone.1..sunk, s32[]{:T(128)} %constant.241.clone.1..sunk) | dynamic-update-slice | bytes 1867780 | tf_op jit(solution)/shard_map/while/body/eval_jaxpr/dynamic_update_slice | solution.py:123
  491.8 10.1 %dynamic_update_slice.8 = f32[4,56,12,152]{3,1,2,0:T(8,128)} dynamic-update-slice(f32[4,56,12,152]{3,1,2,0:T(8,128)} %get-tuple-element.502, f32[4,32,12,152]{3,1,2,0:T(8,128)S(1)} %bitcast_add_fusion.2, s32[]{:T(128)} %constant.241.clone.1..sunk, s32[]{:T(128)} %get-tuple-element.501, s32[]{:T(128)} %constant.241.clone.1..sunk, s32[]{:T(128)} %constant.241.clone.1..sunk) | dynamic-update-slice | bytes 1867780 | tf_op jit(solution)/shard_map/while/body/eval_jaxpr/dynamic_update_slice | solution.py:123
  505.0 10.1 %dynamic_update_slice.8 = f32[4,56,12,152]{3,1,2,0:T(8,128)} dynamic-update-slice(f32[4,56,12,152]{3,1,2,0:T(8,128)} %get-tuple-element.502, f32[4,32,12,152]{3,1,2,0:T(8,128)S(1)} %bitcast_add_fusion.2, s32[]{:T(128)} %constant.241.clone.1..sunk, s32[]{:T(128)} %get-tuple-element.501, s32[]{:T(128)} %constant.241.clone.1..sunk, s32[]{:T(128)} %constant.241.clone.1..sunk) | dynamic-update-slice | bytes 1867780 | tf_op jit(solution)/shard_map/while/body/eval_jaxpr/dynamic_update_slice | solution.py:123
  518.3 10.1 %dynamic_update_slice.8 = f32[4,56,12,152]{3,1,2,0:T(8,128)} dynamic-update-slice(f32[4,56,12,152]{3,1,2,0:T(8,128)} %get-tuple-element.502, f32[4,32,12,152]{3,1,2,0:T(8,128)S(1)} %bitcast_add_fusion.2, s32[]{:T(128)} %constant.241.clone.1..sunk, s32[]{:T(128)} %get-tuple-element.501, s32[]{:T(128)} %constant.241.clone.1..sunk, s32[]{:T(128)} %constant.241.clone.1..sunk) | dynamic-update-slice | bytes 1867780 | tf_op jit(solution)/shard_map/while/body/eval_jaxpr/dynamic_update_slice | solution.py:123
  531.6 10.1 %dynamic_update_slice.8 = f32[4,56,12,152]{3,1,2,0:T(8,128)} dynamic-update-slice(f32[4,56,12,152]{3,1,2,0:T(8,128)} %get-tuple-element.502, f32[4,32,12,152]{3,1,2,0:T(8,128)S(1)} %bitcast_add_fusion.2, s32[]{:T(128)} %constant.241.clone.1..sunk, s32[]{:T(128)} %get-tuple-element.501, s32[]{:T(128)} %constant.241.clone.1..sunk, s32[]{:T(128)} %constant.241.clone.1..sunk) | dynamic-update-slice | bytes 1867780 | tf_op jit(solution)/shard_map/while/body/eval_jaxpr/dynamic_update_slice | solution.py:123
  544.8 10.1 %dynamic_update_slice.8 = f32[4,56,12,152]{3,1,2,0:T(8,128)} dynamic-update-slice(f32[4,56,12,152]{3,1,2,0:T(8,128)} %get-tuple-element.502, f32[4,32,12,152]{3,1,2,0:T(8,128)S(1)} %bitcast_add_fusion.2, s32[]{:T(128)} %constant.241.clone.1..sunk, s32[]{:T(128)} %get-tuple-element.501, s32[]{:T(128)} %constant.241.clone.1..sunk, s32[]{:T(128)} %constant.241.clone.1..sunk) | dynamic-update-slice | bytes 1867780 | tf_op jit(solution)/shard_map/while/body/eval_jaxpr/dynamic_update_slice | solution.py:123
  558.1 10.1 %dynamic_update_slice.8 = f32[4,56,12,152]{3,1,2,0:T(8,128)} dynamic-update-slice(f32[4,56,12,152]{3,1,2,0:T(8,128)} %get-tuple-element.502, f32[4,32,12,152]{3,1,2,0:T(8,128)S(1)} %bitcast_add_fusion.2, s32[]{:T(128)} %constant.241.clone.1..sunk, s32[]{:T(128)} %get-tuple-element.501, s32[]{:T(128)} %constant.241.clone.1..sunk, s32[]{:T(128)} %constant.241.clone.1..sunk) | dynamic-update-slice | bytes 1867780 | tf_op jit(solution)/shard_map/while/body/eval_jaxpr/dynamic_update_slice | solution.py:123
  571.4 10.1 %dynamic_update_slice.8 = f32[4,56,12,152]{3,1,2,0:T(8,128)} dynamic-update-slice(f32[4,56,12,152]{3,1,2,0:T(8,128)} %get-tuple-element.502, f32[4,32,12,152]{3,1,2,0:T(8,128)S(1)} %bitcast_add_fusion.2, s32[]{:T(128)} %constant.241.clone.1..sunk, s32[]{:T(128)} %get-tuple-element.501, s32[]{:T(128)} %constant.241.clone.1..sunk, s32[]{:T(128)} %constant.241.clone.1..sunk) | dynamic-update-slice | bytes 1867780 | tf_op jit(solution)/shard_map/while/body/eval_jaxpr/dynamic_update_slice | solution.py:123
  584.6 10.1 %dynamic_update_slice.8 = f32[4,56,12,152]{3,1,2,0:T(8,128)} dynamic-update-slice(f32[4,56,12,152]{3,1,2,0:T(8,128)} %get-tuple-element.502, f32[4,32,12,152]{3,1,2,0:T(8,128)S(1)} %bitcast_add_fusion.2, s32[]{:T(128)} %constant.241.clone.1..sunk, s32[]{:T(128)} %get-tuple-element.501, s32[]{:T(128)} %constant.241.clone.1..sunk, s32[]{:T(128)} %constant.241.clone.1..sunk) | dynamic-update-slice | bytes 1867780 | tf_op jit(solution)/shard_map/while/body/eval_jaxpr/dynamic_update_slice | solution.py:123
  597.7 9.6 %dynamic_update_slice.8 = f32[4,56,12,152]{3,1,2,0:T(8,128)} dynamic-update-slice(f32[4,56,12,152]{3,1,2,0:T(8,128)} %get-tuple-element.502, f32[4,32,12,152]{3,1,2,0:T(8,128)S(1)} %bitcast_add_fusion.2, s32[]{:T(128)} %constant.241.clone.1..sunk, s32[]{:T(128)} %get-tuple-element.501, s32[]{:T(128)} %constant.241.clone.1..sunk, s32[]{:T(128)} %constant.241.clone.1..sunk) | dynamic-update-slice | bytes 1867780 | tf_op jit(solution)/shard_map/while/body/eval_jaxpr/dynamic_update_slice | solution.py:123
  626.9 29.9 %while.33 = (s32[]{:T(128)}, bf16[4,32,2048]{2,1,0:T(8,128)(2,1)S(1)}, s32[4,3]{1,0:T(4,128)S(1)}, bf16[4,32,1560]{2,1,0:T(8,128)(2,1)S(1)}, s32[]{:T(128)}, /*index=5*/s32[3]{0:T(128)S(1)}, s32[]{:T(128)}) while((s32[]{:T(128)}, bf16[4,32,2048]{2,1,0:T(8,128)(2,1)S(1)}, s32[4,3]{1,0:T(4,128)S(1)}, bf16[4,32,1560]{2,1,0:T(8,128)(2,1)S(1)}, ...), condition=%wide.while_cond.3, body=%wide.while_body.3.sunk | while | flops 49939 | bytes 499371 | solution.py:145
  661.9 8.8 %all-to-all-start.2 = ((bf16[16,4,32,512]{3,2,1,0:T(8,128)(2,1)}), bf16[16,4,32,512]{3,2,1,0:T(8,128)(2,1)S(1)}, u32[]{:S(2)}, u32[]{:S(2)}) async-start(bf16[16,4,32,512]{3,2,1,0:T(8,128)(2,1)} %broadcast_select_fusion.1), calls=%async_computation.2 | async-start | bytes 4194304 | tf_op jit(solution)/shard_map/all_to_all | solution.py:156
  670.8 22.7 %all-to-all-done.2 = bf16[16,4,32,512]{3,2,1,0:T(8,128)(2,1)S(1)} async-done(((bf16[16,4,32,512]{3,2,1,0:T(8,128)(2,1)}), bf16[16,4,32,512]{3,2,1,0:T(8,128)(2,1)S(1)}, u32[]{:S(2)}, u32[]{:S(2)}) %all-to-all-start.2) | async-done | bytes 2097184 | tf_op jit(solution)/shard_map/all_to_all | solution.py:156
  696.0 10.2 %all-to-all-start.3 = ((bf16[8,4,32,512]{3,2,1,0:T(8,128)(2,1)}), bf16[8,4,32,512]{3,2,1,0:T(8,128)(2,1)S(1)}, u32[]{:S(2)}, u32[]{:S(2)}) async-start(bf16[8,4,32,512]{3,2,1,0:T(8,128)(2,1)} %copy.152), calls=%async_computation.3 | async-start | bytes 2097152 | tf_op jit(solution)/shard_map/all_to_all | solution.py:163
  706.2 15.1 %all-to-all-done.3 = bf16[8,4,32,512]{3,2,1,0:T(8,128)(2,1)S(1)} async-done(((bf16[8,4,32,512]{3,2,1,0:T(8,128)(2,1)}), bf16[8,4,32,512]{3,2,1,0:T(8,128)(2,1)S(1)}, u32[]{:S(2)}, u32[]{:S(2)}) %all-to-all-start.3) | async-done | bytes 1048608 | tf_op jit(solution)/shard_map/all_to_all | solution.py:163
  725.5 7.0 scatter_fusion
  (225 shorter events, 312.6 us)
Async XLA Ops:
  0.0 7.9 %copy-start = (bf16[64,32,512]{2,1,0:T(8,128)(2,1)S(1)}, bf16[64,32,512]{2,1,0:T(8,128)(2,1)}, u32[]{:S(2)}) copy-start(bf16[64,32,512]{2,1,0:T(8,128)(2,1)} %param.16) | copy-start | bytes 6291460
  9.6 21.9 %all-to-all-start = ((bf16[8,4,32,512]{3,2,1,0:T(8,128)(2,1)}), bf16[8,4,32,512]{3,2,1,0:T(8,128)(2,1)S(1)}, u32[]{:S(2)}, u32[]{:S(2)}) async-start(bf16[8,4,32,512]{3,2,1,0:T(8,128)(2,1)} %broadcast_select_fusion.2), calls=%async_computation | async-start | bytes 2097152 | tf_op jit(solution)/shard_map/all_to_all | solution.py:58
  37.2 7.1 copy-start.7
  37.3 33.4 %all-to-all-start.1 = ((bf16[16,4,32,512]{3,2,1,0:T(8,128)(2,1)}), bf16[16,4,32,512]{3,2,1,0:T(8,128)(2,1)S(1)}, u32[]{:S(2)}, u32[]{:S(2)}) async-start(bf16[16,4,32,512]{3,2,1,0:T(8,128)(2,1)} %broadcast_select_fusion), calls=%async_computation.1 | async-start | bytes 4194304 | tf_op jit(solution)/shard_map/all_to_all | solution.py:65
  65.3 5.3 copy-start.9
  71.2 9.9 %copy-start.4 = (bf16[4,56,1560]{2,1,0:T(8,128)(2,1)S(1)}, bf16[4,56,1560]{2,1,0:T(8,128)(2,1)}, u32[]{:S(2)}) copy-start(bf16[4,56,1560]{2,1,0:T(8,128)(2,1)} %custom-call.21) | copy-start | bytes 2096644
  71.3 5.6 collective-permute-start
  73.7 7.1 collective-permute-start.1
  247.2 4.0 copy-start.5
  247.2 4.0 copy-start.6
  251.2 1.7 copy-start.3
  607.4 2.2 copy-start.2
  613.0 4.8 copy-start.10
  614.3 6.1 collective-permute-start.2
  619.2 6.6 collective-permute-start.3
  621.6 5.2 copy-start.8
  661.9 31.6 %all-to-all-start.2 = ((bf16[16,4,32,512]{3,2,1,0:T(8,128)(2,1)}), bf16[16,4,32,512]{3,2,1,0:T(8,128)(2,1)S(1)}, u32[]{:S(2)}, u32[]{:S(2)}) async-start(bf16[16,4,32,512]{3,2,1,0:T(8,128)(2,1)} %broadcast_select_fusion.1), calls=%async_computation.2 | async-start | bytes 4194304 | tf_op jit(solution)/shard_map/all_to_all | solution.py:156
  696.0 25.4 %all-to-all-start.3 = ((bf16[8,4,32,512]{3,2,1,0:T(8,128)(2,1)}), bf16[8,4,32,512]{3,2,1,0:T(8,128)(2,1)S(1)}, u32[]{:S(2)}, u32[]{:S(2)}) async-start(bf16[8,4,32,512]{3,2,1,0:T(8,128)(2,1)} %copy.152), calls=%async_computation.3 | async-start | bytes 2097152 | tf_op jit(solution)/shard_map/all_to_all | solution.py:163
  722.9 9.5 %copy-start.1 = (bf16[64,32,512]{2,1,0:T(8,128)(2,1)S(1)}, bf16[64,32,512]{2,1,0:T(8,128)(2,1)}, u32[]{:S(2)}) copy-start(bf16[64,32,512]{2,1,0:T(8,128)(2,1)} %param.16) | copy-start | bytes 6291460
where the time goes:
time: 742 us; the launch traced here: 732 us
  local copies, waits for them, and re-layouts  362 us (49%)
  matrix products  217 us (29%)
  waiting for transfers between devices  64.3 us (9%)
  other arithmetic  47.4 us (6%)
  starting transfers between devices  41 us (6%)
    dynamic_update_slice x25, local copies, waits for them, and re-layouts, adjoint_step(): lax.dynamic_update_slice_in_dim(growing, current + term, kernel_row, 1)  254 us
    dot_general x25, matrix products, forward_step(): jnp.einsum('eykc,cn->eykn', rows, table, preferred_element_type=jnp.float32)  135 us
    dot_general x25, matrix products, adjoint_step(): jnp.einsum('eykn,cn->eykc', spread, table, preferred_element_type=jnp.flo...  79.5 us
    all_to_all x1, waiting for transfers between devices, local(): lax.all_to_all(to_rows, 'pix', split_axis=0, concat_axis=0, tiled=True)  22.7 us
    scatter x8, other arithmetic  18.6 us
    all_to_all x1, waiting for transfers between devices, local(): lax.all_to_all(to_owners, 'exp', split_axis=0, concat_axis=0, tiled=True)  15.1 us
  transfers between devices with their start and end apart: 8, of which 7 were waited for; matrix products, arithmetic and copies ran while one was open for 4% of the time, Pallas kernels for 0%

commit v1 on v0

v1 whole, which is shorter than its diff:
```python
import jax
import jax.numpy as jnp
from jax import lax
from jax.experimental import pallas as pl
from jax.experimental.pallas import tpu as pltpu
from jax.sharding import PartitionSpec as P


KS = 25
def tables(kernels):
    nb, ks, _ = kernels.shape
    rows, tall = 32, 64
    u = jnp.arange(ks)[:, None, None]; Y = jnp.arange(tall)[None, :, None]; y = jnp.arange(rows)[None, None, :]
    hot = (Y - 4 - y == u).astype(kernels.dtype)
    t = jnp.einsum("buv,uYy->bvYy", kernels, hot, preferred_element_type=jnp.float32).astype(kernels.dtype)
    fwd = t.transpose(0, 3, 1, 2).reshape(nb * rows, ks * tall)
    adj = t.reshape(nb, 5, 5, tall, rows).transpose(1, 3, 2, 0, 4).reshape(5 * tall, 5 * nb * rows)
    return fwd, adj

def blur_kernel(shift_ref, band_ref, coef_ref, obs_ref, inv_ref, fwd_ref, adj_ref, out_ref, stack, wide):
    q = pl.program_id(0)
    shift = shift_ref[q]
    W = 1536
    band = band_ref[0].astype(jnp.float32)
    width = band.shape[1]
    win = pltpu.roll(band, (width - shift) % width, axis=1)[:, :1664].astype(jnp.bfloat16)
    for v in range(KS):
        stack[v*64:(v+1)*64, :] = win[:, v:v+W]
    nc = 512
    for n in range(W // nc):
        cols = slice(n*nc, (n+1)*nc)
        blurred = jnp.dot(fwd_ref[...], stack[:, cols], preferred_element_type=jnp.float32)
        coef = [coef_ref[0, b, :, cols].astype(jnp.float32) for b in range(6)]
        model = coef[0] * blurred[0:32]
        for b in range(1, 6):
            model = model + coef[b] * blurred[b*32:(b+1)*32]
        resid = inv_ref[0, :, cols].astype(jnp.float32) * (model - obs_ref[0, :, cols])
        for b in range(6):
            wide[b*32:(b+1)*32, cols] = (coef[b] * resid).astype(jnp.bfloat16)
    wide[0:192, W:] = jnp.zeros((192, 128), jnp.bfloat16)
    base = wide[0:192, :]
    for c in range(1, 5):
        wide[c*192:(c+1)*192, :] = jnp.concatenate([jnp.zeros((192, c), jnp.bfloat16), base[:, :1664-c]], axis=1)
    part = jnp.dot(adj_ref[...], wide[...], preferred_element_type=jnp.float32)
    back = part[0:64]
    for a in range(1, 5):
        back = back + pltpu.roll(part[a*64:(a+1)*64], 5*a, axis=1)
    back = jnp.concatenate([back, jnp.zeros((64, width - 1664), jnp.float32)], axis=1)
    out_ref[0] = pltpu.roll(back, shift, axis=1).astype(out_ref.dtype)

def blur(shift, band, coefs, observed, inv_var, fwd, adj, out_dtype=jnp.float32):
    nv = band.shape[0]
    whole = lambda a: pl.BlockSpec(a.shape, lambda q, s: (0,)*a.ndim)
    per = lambda a: pl.BlockSpec((1,)+a.shape[1:], lambda q, s: (q,)+(0,)*(a.ndim-1))
    return pl.pallas_call(
        blur_kernel,
        grid_spec=pltpu.PrefetchScalarGridSpec(
            num_scalar_prefetch=1, grid=(nv,),
            in_specs=[per(band), per(coefs), per(observed), per(inv_var), whole(fwd), whole(adj)],
            out_specs=pl.BlockSpec((1,64,2048), lambda q, s: (q,0,0)),
            scratch_shapes=[pltpu.VMEM((1600,1536), jnp.bfloat16), pltpu.VMEM((960,1664), jnp.bfloat16)]),
        out_shape=jax.ShapeDtypeStruct((nv,64,2048), out_dtype),
        compiler_params=pltpu.CompilerParams(vmem_limit_bytes=50*2**20),
    )(shift, band, coefs, observed, inv_var, fwd, adj)


def with_halo(block, sides, width):
    for axis, dim in sides:
        count = lax.axis_size(axis)
        forward = [(i, i + 1) for i in range(count - 1)]
        backward = [(target, source) for source, target in forward]
        low = lax.ppermute(
            lax.slice_in_dim(block, block.shape[dim] - width, None, axis=dim), axis, forward
        )
        high = lax.ppermute(lax.slice_in_dim(block, 0, width, axis=dim), axis, backward)
        block = jnp.concatenate([low, block, high], axis=dim)
    return block


def passed_along(x, axis, by):
    peers = lax.axis_size(axis)
    pairs = [(i, i + by) for i in range(peers) if 0 <= i + by < peers]
    return lax.ppermute(x, axis, pairs)


def owned_rows(tiles, owner_of, local_of, group_index):
    belongs = owner_of[tiles] == group_index
    which = jnp.argmax(belongs.astype(jnp.int32), axis=-1)
    chosen = jnp.take_along_axis(tiles, which[..., None], axis=-1)[..., 0]
    return (local_of[chosen], jnp.any(belongs, axis=-1))


def local(sky, kernels, coefs, observed, inv_var, footprints, offsets, tile_slot):
    group_count = lax.axis_size("exp")
    strip_count = lax.axis_size("pix")
    group_index = lax.axis_index("exp")
    strip_index = lax.axis_index("pix")
    stored, strip_rows, tile_side = sky.shape
    visits = observed.shape[0]
    image_width = observed.shape[2]
    kernel_side = kernels.shape[1]
    basis_count = kernels.shape[0]
    margin = kernel_side // 2
    owner_of = tile_slot // stored
    local_of = tile_slot % stored
    blocks = footprints.reshape(group_count, visits, 2, 4)
    phases = (offsets[:, 0] // strip_rows).reshape(group_count, visits)
    shifts = offsets[:, 1].reshape(group_count, visits)
    my_phase = phases[group_index]
    my_shift = shifts[group_index]
    visit_range = jnp.arange(visits)
    strip_range = jnp.arange(strip_count)
    nothing = jnp.zeros((), sky.dtype)
    lower_row = strip_index < phases
    row_tiles = jnp.where(lower_row[..., None], blocks[:, :, 1], blocks[:, :, 0])
    held_rows, held = owned_rows(row_tiles, owner_of, local_of, group_index)
    outgoing = jnp.where(held[..., None, None], sky[held_rows], nothing)
    arrived = lax.all_to_all(outgoing, "exp", split_axis=0, concat_axis=0, tiled=True)
    source = owner_of[row_tiles[group_index]]
    picked = arrived[source, visit_range[:, None]]
    matching = (my_phase[None, :] + strip_range[:, None]) % strip_count == strip_index
    chosen = jnp.argmax(matching.astype(jnp.int32), axis=1)
    present = jnp.any(matching, axis=1)
    forward_rows = jnp.where(present[:, None, None, None], picked[chosen], nothing)
    landed = lax.all_to_all(forward_rows, "pix", split_axis=0, concat_axis=0, tiled=True)
    mine = landed[(my_phase + strip_index) % strip_count]
    band = mine.transpose(0, 2, 1, 3).reshape(visits, strip_rows, 4 * tile_side)
    padded = with_halo(band, (("pix", 1),), 16)

    fwd, adj = tables(kernels)
    back = blur(my_shift - margin, padded, coefs, observed, inv_var, fwd, adj)
    from_lower = passed_along(back[:, 48:].astype(jnp.bfloat16), "pix", 1).astype(jnp.float32)
    from_upper = passed_along(back[:, :16].astype(jnp.bfloat16), "pix", -1).astype(jnp.float32)
    placed = back[:, 16:48] + jnp.concatenate([from_lower, from_upper], axis=1)
    pieces = (
        placed.reshape(visits, strip_rows, 4, tile_side).transpose(0, 2, 1, 3).astype(jnp.bfloat16)
    )
    gradient = jnp.zeros((stored, strip_rows, tile_side), jnp.float32)
    back_match = (my_phase[None, :] + strip_index) % strip_count == strip_range[:, None]
    back_visit = jnp.argmax(back_match.astype(jnp.int32), axis=1)
    back_has = jnp.any(back_match, axis=1)
    to_rows = jnp.where(back_has[:, None, None, None], pieces[back_visit], nothing)
    gathered = lax.all_to_all(to_rows, "pix", split_axis=0, concat_axis=0, tiled=True)
    per_visit = gathered[(strip_index - my_phase) % strip_count]
    owners_row = owner_of[row_tiles[group_index]]
    selector = (owners_row[None] == jnp.arange(group_count)[:, None, None]).astype(jnp.bfloat16)
    to_owners = jnp.einsum(
        "gqj,qjst->gqst", selector, per_visit, preferred_element_type=jnp.float32
    ).astype(jnp.bfloat16)
    returned = lax.all_to_all(to_owners, "exp", split_axis=0, concat_axis=0, tiled=True)
    terms = jnp.where(held[..., None, None], returned.astype(jnp.float32), 0.0)
    gradient = gradient.at[held_rows.reshape(-1)].add(terms.reshape(-1, strip_rows, tile_side))
    return gradient


def solution(mesh):
    return jax.shard_map(
        local,
        mesh=mesh,
        in_specs=(
            P("exp", "pix", None),
            P(),
            P("exp", None, "pix", None),
            P("exp", "pix", None),
            P("exp", "pix", None),
            P(),
            P(),
            P(),
        ),
        out_specs=P("exp", "pix", None),
        check_vma=False,
    )
```

time: 742 us -> 203 us (0.27); the launches traced: 732 us -> 202 us
  local copies, waits for them, and re-layouts: 362 us -> 33.7 us
  matrix products: 217 us -> 2.34 us
  other arithmetic: 47.4 us -> 22.7 us
  Pallas kernels: 0 us -> 18 us
  waiting for transfers between devices: 64.3 us -> 81.9 us
    dynamic_update_slice x25 -> x0, local copies, waits for them, and re-layouts: 254 us -> none  [adjoint_step(): lax.dynamic_update_slice_in_dim(growing, current + term, kernel_row, 1)]
    dot_general x51 -> x1, matrix products: 216 us -> 1.76 us  [tables(): jnp.einsum('buv,uYy->bvYy', kernels, hot, preferred_element_type=jnp.floa...]
    reshape x9 -> x3, local copies, waits for them, and re-layouts: 40.5 us -> 5.34 us  [the longest x2 3.08 us: tables(): t.reshape(nb, 5, 5, tall, rows).transpose(1, 3, 2, 0, 4)]
    all_to_all x1, waiting for transfers between devices: 4.74 us -> 24.6 us  [local(): lax.all_to_all(forward_rows, 'pix', split_axis=0, concat_axis=0, tiled=True)]
    scatter x8 -> x0, other arithmetic: 18.6 us -> none
    pallas_call x0 -> x1, Pallas kernels: none -> 18 us  [blur(): pl.pallas_call(blur_kernel, grid_spec=pltpu.PrefetchScalarGridSpec(num_sc...]
    transpose x2 -> x1, local copies, waits for them, and re-layouts: 13.4 us -> 1.91 us  [tables(): t.reshape(nb, 5, 5, tall, rows).transpose(1, 3, 2, 0, 4)]
    scatter x12 -> x0, local copies, waits for them, and re-layouts: 11.1 us -> none
  transfers between devices with their start and end apart: 8 -> 8, of which waited for: 7 -> 6; matrix products, arithmetic and copies ran while one was open for 4% -> 8% of each run, Pallas kernels for 0% -> 0%
where the time goes in v1:
time: 203 us; the launch traced here: 202 us
  waiting for transfers between devices  81.9 us (40%)
  starting transfers between devices  42.6 us (21%)
  local copies, waits for them, and re-layouts  33.7 us (17%)
  other arithmetic  22.7 us (11%)
  Pallas kernels  18 us (9%)
  matrix products  2.34 us (1%)
    all_to_all x1, waiting for transfers between devices, local(): lax.all_to_all(forward_rows, 'pix', split_axis=0, concat_axis=0, tiled=True)  24.6 us
    all_to_all x1, waiting for transfers between devices, local(): lax.all_to_all(to_rows, 'pix', split_axis=0, concat_axis=0, tiled=True)  23.2 us
    pallas_call x1, Pallas kernels, blur(): pl.pallas_call(blur_kernel, grid_spec=pltpu.PrefetchScalarGridSpec(num_sc...  18 us
    all_to_all x1, waiting for transfers between devices, local(): lax.all_to_all(to_owners, 'exp', split_axis=0, concat_axis=0, tiled=True)  15.1 us
    all_to_all x1, waiting for transfers between devices, local(): lax.all_to_all(outgoing, 'exp', split_axis=0, concat_axis=0, tiled=True)  13.2 us
    all_to_all x1, starting transfers between devices, local(): lax.all_to_all(to_owners, 'exp', split_axis=0, concat_axis=0, tiled=True)  9.89 us
    all_to_all x1, starting transfers between devices, local(): lax.all_to_all(to_rows, 'pix', split_axis=0, concat_axis=0, tiled=True)  9.53 us
    scatter-add x1, other arithmetic, local(): gradient.at[held_rows.reshape(-1)]  6.95 us
  transfers between devices with their start and end apart: 8, of which 6 were waited for; matrix products, arithmetic and copies ran while one was open for 8% of the time, Pallas kernels for 0%

profile of v1, /device:TPU:1, one launch (start us, length us, event | category | flops | bytes accessed | tf_op | source)
XLA Modules:
  0.0 201.6 jit_solution(6249526861217183914)
XLA Ops:
  0.0 0.9 slice_reduce_fusion
  1.1 0.8 reshape.328
  2.1 0.7 add_select_fusion.2
  3.0 1.3 gather_fusion
  4.4 1.0 iota_reduce_fusion
  5.8 0.8 gather_fusion.9
  6.8 0.7 gather_fusion.1
  7.9 0.6 gather_fusion.2
  8.5 1.1 broadcast_select_fusion.2
  9.6 6.8 %all-to-all-start = ((bf16[8,4,32,512]{3,2,1,0:T(8,128)(2,1)}), bf16[8,4,32,512]{3,2,1,0:T(8,128)(2,1)}, u32[]{:S(2)}, u32[]{:S(2)}) async-start(bf16[8,4,32,512]{3,2,1,0:T(8,128)(2,1)} %broadcast_select_fusion.2), calls=%async_computation | async-start | bytes 2097152 | tf_op jit(solution)/shard_map/all_to_all | solution.py:118
  16.8 0.7 gather_fusion.3
  17.6 0.7 iota_reduce_fusion.2
  18.4 13.2 %all-to-all-done = bf16[8,4,32,512]{3,2,1,0:T(8,128)(2,1)} async-done(((bf16[8,4,32,512]{3,2,1,0:T(8,128)(2,1)}), bf16[8,4,32,512]{3,2,1,0:T(8,128)(2,1)}, u32[]{:S(2)}, u32[]{:S(2)}) %all-to-all-start) | async-done | bytes 1048608 | tf_op jit(solution)/shard_map/all_to_all | solution.py:118
  31.7 1.8 gather_fusion.4
  33.5 2.0 gather_fusion.5
  35.5 3.1 %broadcast_select_fusion = bf16[16,4,32,512]{3,2,1,0:T(8,128)(2,1)} fusion(bf16[16,4,32,512]{3,2,1,0:T(8,128)(2,1)} %gather_fusion.5, pred[16]{0:T(512)(128)(4,1)S(1)} %fusion.33), kind=kLoop, calls=%fused_computation.12 | loop fusion | flops 1048576 | bytes 4194320 | tf_op jit(solution)/shard_map/jit(_where)/select_n | solution.py:124
  38.6 6.9 %all-to-all-start.1 = ((bf16[16,4,32,512]{3,2,1,0:T(8,128)(2,1)}), bf16[16,4,32,512]{3,2,1,0:T(8,128)(2,1)}, u32[]{:S(2)}, u32[]{:S(2)}) async-start(bf16[16,4,32,512]{3,2,1,0:T(8,128)(2,1)} %broadcast_select_fusion), calls=%async_computation.1 | async-start | bytes 4194304 | tf_op jit(solution)/shard_map/all_to_all | solution.py:125
  45.7 1.8 convolution_convert_fusion
  47.4 24.6 %all-to-all-done.1 = bf16[16,4,32,512]{3,2,1,0:T(8,128)(2,1)} async-done(((bf16[16,4,32,512]{3,2,1,0:T(8,128)(2,1)}), bf16[16,4,32,512]{3,2,1,0:T(8,128)(2,1)}, u32[]{:S(2)}, u32[]{:S(2)}) %all-to-all-start.1) | async-done | bytes 2097184 | tf_op jit(solution)/shard_map/all_to_all | solution.py:125
  72.1 2.2 %gather_fusion.6 = bf16[4,4,32,512]{3,2,1,0:T(8,128)(2,1)S(1)} fusion(bf16[16,4,32,512]{3,2,1,0:T(8,128)(2,1)} %all-to-all-done.1, s32[1024]{0:T(1024)S(1)} %pad_clamp_fusion.2), kind=kCustom, calls=%fused_computation.6 | custom fusion | bytes 1048592 | tf_op jit(solution)/shard_map/gather | solution.py:126
  74.3 0.8 fusion.35
  75.1 2.9 %collective-permute-start = (bf16[4,16,2048]{2,1,0:T(8,128)(2,1)}, bf16[4,16,2048]{2,1,0:T(8,128)(2,1)}, u32[]{:S(2)}, u32[]{:S(2)}) collective-permute-start(bf16[4,16,2048]{2,1,0:T(8,128)(2,1)} %get-tuple-element.19), channel_id=1, source_target_pairs={{0,1},{1,2},{2,3},{3,4},{4,5},{5,6},{6,7},{7,8},{8,9},{9,10},{10,1... | collective-permute-start | bytes 786440 | tf_op jit(solution)/shard_map/ppermute | solution.py:72
  78.0 1.3 collective-permute-start.1
  79.4 0.8 copy.129
  80.2 1.9 copy.130
  82.1 2.8 %reshape.334 = bf16[320,960]{0,1:T(8,128)(2,1)S(1)} reshape(bf16[5,64,5,6,32]{1,0,4,3,2:T(8,128)(2,1)} %copy.130) | data formatting | bytes 1228800 | tf_op jit(solution)/shard_map/reshape | solution.py:17
  85.2 2.9 %copy.128 = bf16[6,32,25,64]{3,2,1,0:T(8,128)(2,1)} copy(bf16[6,32,25,64]{3,2,0,1:T(8,128)(2,1)} %bitcast.79) | data formatting | bytes 1228800 | tf_op jit(solution)/shard_map/convert_element_type | solution.py:15
  88.1 2.3 %reshape.332.fwd_ref = bf16[192,1600]{1,0:T(8,128)(2,1)S(1)} reshape(bf16[6,32,25,64]{3,2,1,0:T(8,128)(2,1)} %copy.128) | data formatting | bytes 1228800 | tf_op jit(solution)/shard_map/reshape | solution.py:16
  90.4 0.6 iota_reduce_fusion.1
  91.0 1.3 pad_maximum_fusion.band_ref
  92.3 18.0 %shard_map.82 = f32[4,64,2048]{2,1,0:T(8,128)} custom-call(s32[4]{0:T(128)S(1)} %fusion.25.shift_ref, bf16[4,64,2048]{2,1,0:T(8,128)(2,1)S(1)} %pad_maximum_fusion.band_ref, bf16[4,6,32,1536]{3,2,1,0:T(8,128)(2,1)} %coef_ref.1, f32[4,32,1536]{2,1,0:T(8,128)S(1)} %copy-done.1, bf16[4,32,1536]{2,1,0:T(8,128)(2,1)S(1)} %copy-done.2, ...), custom_call_target="tpu_custom_call" | custom-call | tf_op jit(solution)/shard_map/pallas_call | solution.py:55
  110.3 1.9 convert.5
  112.3 4.0 %collective-permute-start.2 = (bf16[4,16,2048]{2,1,0:T(8,128)(2,1)S(1)}, bf16[4,16,2048]{2,1,0:T(8,128)(2,1)S(1)}, u32[]{:S(2)}, u32[]{:S(2)}) collective-permute-start(bf16[4,16,2048]{2,1,0:T(8,128)(2,1)S(1)} %get-tuple-element.17), channel_id=1, source_target_pairs={{0,1},{1,2},{2,3},{3,4},{4,5},{5,6},{6,7},{7,8},{8,9},{9,10},{10,1... | collective-permute-start | bytes 786440 | tf_op jit(solution)/shard_map/ppermute | solution.py:83
  116.3 1.3 collective-permute-start.3
  117.7 1.9 collective-permute-done.2
  119.5 3.8 %collective-permute-done.3 = bf16[4,16,2048]{2,1,0:T(8,128)(2,1)S(1)} collective-permute-done((bf16[4,16,2048]{2,1,0:T(8,128)(2,1)S(1)}, bf16[4,16,2048]{2,1,0:T(8,128)(2,1)S(1)}, u32[]{:S(2)}, u32[]{:S(2)}) %collective-permute-start.3) | collective-permute-done | bytes 262176 | tf_op jit(solution)/shard_map/ppermute | solution.py:83
  123.6 2.0 gather_fusion.7
  125.6 3.1 %broadcast_select_fusion.1 = bf16[16,4,32,512]{3,2,1,0:T(8,128)(2,1)} fusion(bf16[16,4,32,512]{3,2,1,0:T(8,128)(2,1)} %gather_fusion.7, pred[16]{0:T(512)(128)(4,1)S(1)} %fusion.22), kind=kLoop, calls=%fused_computation.13 | loop fusion | flops 1048576 | bytes 4194320 | tf_op jit(solution)/shard_map/jit(_where)/select_n | solution.py:142
  128.7 9.5 %all-to-all-start.2 = ((bf16[16,4,32,512]{3,2,1,0:T(8,128)(2,1)}), bf16[16,4,32,512]{3,2,1,0:T(8,128)(2,1)}, u32[]{:S(2)}, u32[]{:S(2)}) async-start(bf16[16,4,32,512]{3,2,1,0:T(8,128)(2,1)} %broadcast_select_fusion.1), calls=%async_computation.2 | async-start | bytes 4194304 | tf_op jit(solution)/shard_map/all_to_all | solution.py:143
  138.3 23.2 %all-to-all-done.2 = bf16[16,4,32,512]{3,2,1,0:T(8,128)(2,1)} async-done(((bf16[16,4,32,512]{3,2,1,0:T(8,128)(2,1)}), bf16[16,4,32,512]{3,2,1,0:T(8,128)(2,1)}, u32[]{:S(2)}, u32[]{:S(2)}) %all-to-all-start.2) | async-done | bytes 2097184 | tf_op jit(solution)/shard_map/all_to_all | solution.py:143
  161.5 2.2 %gather_fusion.8 = bf16[4,4,32,512]{3,2,1,0:T(8,128)(2,1)S(1)} fusion(bf16[16,4,32,512]{3,2,1,0:T(8,128)(2,1)} %all-to-all-done.2, s32[1024]{0:T(1024)S(1)} %pad_clamp_fusion), kind=kCustom, calls=%fused_computation.8 | custom fusion | bytes 1048592 | tf_op jit(solution)/shard_map/gather | solution.py:144
  163.7 0.6 fusion
  164.3 1.3 copy.134
  165.6 9.9 %all-to-all-start.3 = ((bf16[8,4,32,512]{3,2,1,0:T(8,128)(2,1)}), bf16[8,4,32,512]{3,2,1,0:T(8,128)(2,1)S(1)}, u32[]{:S(2)}, u32[]{:S(2)}) async-start(bf16[8,4,32,512]{3,2,1,0:T(8,128)(2,1)} %copy.134), calls=%async_computation.3 | async-start | bytes 2097152 | tf_op jit(solution)/shard_map/all_to_all | solution.py:150
  175.5 15.1 %all-to-all-done.3 = bf16[8,4,32,512]{3,2,1,0:T(8,128)(2,1)S(1)} async-done(((bf16[8,4,32,512]{3,2,1,0:T(8,128)(2,1)}), bf16[8,4,32,512]{3,2,1,0:T(8,128)(2,1)S(1)}, u32[]{:S(2)}, u32[]{:S(2)}) %all-to-all-start.3) | async-done | bytes 1048608 | tf_op jit(solution)/shard_map/all_to_all | solution.py:150
  190.6 1.6 convert_select_fusion
  192.1 2.5 %broadcast_in_dim.93 = f32[64,32,512]{2,1,0:T(8,128)} broadcast(f32[]{:T(128)} %constant.121.clone.1), dimensions={} | broadcast | bytes 4194308 | tf_op jit(solution)/shard_map/broadcast_in_dim | solution.py:138
  194.7 6.9 %scatter_fusion = f32[64,32,512]{2,1,0:T(8,128)} fusion(f32[64,32,512]{2,1,0:T(8,128)} %broadcast_in_dim.93, s32[32]{0:T(128)S(1)} %fusion.30, f32[32,32,512]{2,1,0:T(8,128)} %bitcast.83), kind=kCustom, calls=%fused_computation.10 | custom fusion | flops 524288 | bytes 6291584 | tf_op jit(solution)/shard_map/scatter-add | solution.py:152
  (77 shorter events, 3.3 us)
Async XLA Ops:
  0.0 7.9 %copy-start = (bf16[64,32,512]{2,1,0:T(8,128)(2,1)S(1)}, bf16[64,32,512]{2,1,0:T(8,128)(2,1)}, u32[]{:S(2)}) copy-start(bf16[64,32,512]{2,1,0:T(8,128)(2,1)} %param.8) | copy-start | bytes 6291460
  9.6 22.0 %all-to-all-start = ((bf16[8,4,32,512]{3,2,1,0:T(8,128)(2,1)}), bf16[8,4,32,512]{3,2,1,0:T(8,128)(2,1)}, u32[]{:S(2)}, u32[]{:S(2)}) async-start(bf16[8,4,32,512]{3,2,1,0:T(8,128)(2,1)} %broadcast_select_fusion.2), calls=%async_computation | async-start | bytes 2097152 | tf_op jit(solution)/shard_map/all_to_all | solution.py:118
  38.6 7.1 %copy-start.6 = (bf16[6,25,25]{2,1,0:T(8,128)(2,1)S(1)}, bf16[6,25,25]{2,1,0:T(8,128)(2,1)}, u32[]{:S(2)}) copy-start(bf16[6,25,25]{2,1,0:T(8,128)(2,1)} %param.9) | copy-start | bytes 22504
  38.6 33.5 %all-to-all-start.1 = ((bf16[16,4,32,512]{3,2,1,0:T(8,128)(2,1)}), bf16[16,4,32,512]{3,2,1,0:T(8,128)(2,1)}, u32[]{:S(2)}, u32[]{:S(2)}) async-start(bf16[16,4,32,512]{3,2,1,0:T(8,128)(2,1)} %broadcast_select_fusion), calls=%async_computation.1 | async-start | bytes 4194304 | tf_op jit(solution)/shard_map/all_to_all | solution.py:125
  74.2 5.1 %copy-start.3 = (bf16[64,32,6,25]{0,3,2,1:T(8,128)(2,1)S(1)}, bf16[64,32,6,25]{0,3,2,1:T(8,128)(2,1)}, u32[]{:S(2)}) copy-start(bf16[64,32,6,25]{0,3,2,1:T(8,128)(2,1)} %convolution_convert_fusion) | copy-start | bytes 1843204
  74.3 5.1 %copy-start.5 = (bf16[4,4,4,8,512]{4,3,1,2,0:T(8,128)(2,1)}, bf16[4,4,4,8,512]{4,3,1,2,0:T(8,128)(2,1)S(1)}, u32[]{:S(2)}) copy-start(bf16[4,4,4,8,512]{4,3,1,2,0:T(8,128)(2,1)S(1)} %copy.140) | copy-start | bytes 1572868
  75.1 15.8 %collective-permute-start = (bf16[4,16,2048]{2,1,0:T(8,128)(2,1)}, bf16[4,16,2048]{2,1,0:T(8,128)(2,1)}, u32[]{:S(2)}, u32[]{:S(2)}) collective-permute-start(bf16[4,16,2048]{2,1,0:T(8,128)(2,1)} %get-tuple-element.19), channel_id=1, source_target_pairs={{0,1},{1,2},{2,3},{3,4},{4,5},{5,6},{6,7},{7,8},{8,9},{9,10},{10,1... | collective-permute-start | bytes 786440 | tf_op jit(solution)/shard_map/ppermute | solution.py:72
  78.0 12.9 %collective-permute-start.1 = (bf16[4,16,2048]{2,1,0:T(8,128)(2,1)}, bf16[4,16,2048]{2,1,0:T(8,128)(2,1)}, u32[]{:S(2)}, u32[]{:S(2)}) collective-permute-start(bf16[4,16,2048]{2,1,0:T(8,128)(2,1)} %get-tuple-element.20), channel_id=1, source_target_pairs={{1,0},{2,1},{3,2},{4,3},{5,4},{6,5},{7,6},{8,7},{9,8},{10,9},{11,1... | collective-permute-start | bytes 786440 | tf_op jit(solution)/shard_map/ppermute | solution.py:75
  90.3 1.9 copy-start.1
  90.4 1.9 copy-start.2
  110.3 13.1 %copy-start.4 = (f32[4,64,2048]{2,1,0:T(8,128)S(1)}, f32[4,64,2048]{2,1,0:T(8,128)}, u32[]{:S(2)}) copy-start(f32[4,64,2048]{2,1,0:T(8,128)} %shard_map.82) | copy-start | bytes 6291460
  112.3 7.3 %collective-permute-start.2 = (bf16[4,16,2048]{2,1,0:T(8,128)(2,1)S(1)}, bf16[4,16,2048]{2,1,0:T(8,128)(2,1)S(1)}, u32[]{:S(2)}, u32[]{:S(2)}) collective-permute-start(bf16[4,16,2048]{2,1,0:T(8,128)(2,1)S(1)} %get-tuple-element.17), channel_id=1, source_target_pairs={{0,1},{1,2},{2,3},{3,4},{4,5},{5,6},{6,7},{7,8},{8,9},{9,10},{10,1... | collective-permute-start | bytes 786440 | tf_op jit(solution)/shard_map/ppermute | solution.py:83
  116.3 7.1 %collective-permute-start.3 = (bf16[4,16,2048]{2,1,0:T(8,128)(2,1)S(1)}, bf16[4,16,2048]{2,1,0:T(8,128)(2,1)S(1)}, u32[]{:S(2)}, u32[]{:S(2)}) collective-permute-start(bf16[4,16,2048]{2,1,0:T(8,128)(2,1)S(1)} %get-tuple-element.18), channel_id=1, source_target_pairs={{1,0},{2,1},{3,2},{4,3},{5,4},{6,5},{7,6},{8,7},{9,8},{10,9},{11,1... | collective-permute-start | bytes 786440 | tf_op jit(solution)/shard_map/ppermute | solution.py:83
  128.7 32.8 %all-to-all-start.2 = ((bf16[16,4,32,512]{3,2,1,0:T(8,128)(2,1)}), bf16[16,4,32,512]{3,2,1,0:T(8,128)(2,1)}, u32[]{:S(2)}, u32[]{:S(2)}) async-start(bf16[16,4,32,512]{3,2,1,0:T(8,128)(2,1)} %broadcast_select_fusion.1), calls=%async_computation.2 | async-start | bytes 4194304 | tf_op jit(solution)/shard_map/all_to_all | solution.py:143
  165.6 25.0 %all-to-all-start.3 = ((bf16[8,4,32,512]{3,2,1,0:T(8,128)(2,1)}), bf16[8,4,32,512]{3,2,1,0:T(8,128)(2,1)S(1)}, u32[]{:S(2)}, u32[]{:S(2)}) async-start(bf16[8,4,32,512]{3,2,1,0:T(8,128)(2,1)} %copy.134), calls=%async_computation.3 | async-start | bytes 2097152 | tf_op jit(solution)/shard_map/all_to_all | solution.py:150

commit v2 on v1

v2 whole, which is shorter than its diff:
```python
import jax
import jax.numpy as jnp
from jax import lax
from jax.experimental import pallas as pl
from jax.experimental.pallas import tpu as pltpu
from jax.sharding import PartitionSpec as P

KS = 25
def tables(kernels):
    nb, ks, _ = kernels.shape
    rows, tall = 32, 64
    u = jnp.arange(ks)[:, None, None]; Y = jnp.arange(tall)[None, :, None]; y = jnp.arange(rows)[None, None, :]
    hot = (Y - 4 - y == u).astype(kernels.dtype)
    t = jnp.einsum("buv,uYy->bvYy", kernels, hot, preferred_element_type=jnp.float32).astype(kernels.dtype)
    fwd = t.transpose(0, 3, 1, 2).reshape(nb * rows, ks * tall)
    adj = t.reshape(nb, 5, 5, tall, rows).transpose(1, 3, 2, 0, 4).reshape(5 * tall, 5 * nb * rows)
    return fwd, adj

def blur_kernel(shift_ref, band_ref, coef_ref, obs_ref, inv_ref, fwd_ref, adj_ref, out_ref, stack, wide):
    q = pl.program_id(0)
    shift = shift_ref[q]
    W = 1536
    band = band_ref[0].astype(jnp.float32)
    width = band.shape[1]
    win = pltpu.roll(band, (width - shift) % width, axis=1)[:, :1664].astype(jnp.bfloat16)
    for v in range(KS):
        stack[v*64:(v+1)*64, :] = win[:, v:v+W]
    nc = 512
    for n in range(W // nc):
        cols = slice(n*nc, (n+1)*nc)
        blurred = jnp.dot(fwd_ref[...], stack[:, cols], preferred_element_type=jnp.float32)
        coef = [coef_ref[0, b, :, cols].astype(jnp.float32) for b in range(6)]
        model = coef[0] * blurred[0:32]
        for b in range(1, 6):
            model = model + coef[b] * blurred[b*32:(b+1)*32]
        resid = inv_ref[0, :, cols].astype(jnp.float32) * (model - obs_ref[0, :, cols])
        for b in range(6):
            wide[b*32:(b+1)*32, cols] = (coef[b] * resid).astype(jnp.bfloat16)
    wide[0:192, W:] = jnp.zeros((192, 128), jnp.bfloat16)
    base = wide[0:192, :]
    for c in range(1, 5):
        wide[c*192:(c+1)*192, :] = jnp.concatenate([jnp.zeros((192, c), jnp.bfloat16), base[:, :1664-c]], axis=1)
    part = jnp.dot(adj_ref[...], wide[...], preferred_element_type=jnp.float32)
    back = part[0:64]
    for a in range(1, 5):
        back = back + pltpu.roll(part[a*64:(a+1)*64], 5*a, axis=1)
    back = jnp.concatenate([back, jnp.zeros((64, width - 1664), jnp.float32)], axis=1)
    out_ref[0] = pltpu.roll(back, shift, axis=1).astype(out_ref.dtype)

def blur(shift, band, coefs, observed, inv_var, fwd, adj, out_dtype=jnp.float32):
    nv = band.shape[0]
    whole = lambda a: pl.BlockSpec(a.shape, lambda q, s: (0,)*a.ndim)
    per = lambda a: pl.BlockSpec((1,)+a.shape[1:], lambda q, s: (q,)+(0,)*(a.ndim-1))
    return pl.pallas_call(
        blur_kernel,
        grid_spec=pltpu.PrefetchScalarGridSpec(
            num_scalar_prefetch=1, grid=(nv,),
            in_specs=[per(band), per(coefs), per(observed), per(inv_var), whole(fwd), whole(adj)],
            out_specs=pl.BlockSpec((1,64,2048), lambda q, s: (q,0,0)),
            scratch_shapes=[pltpu.VMEM((1600,1536), jnp.bfloat16), pltpu.VMEM((960,1664), jnp.bfloat16)]),
        out_shape=jax.ShapeDtypeStruct((nv,64,2048), out_dtype),
        compiler_params=pltpu.CompilerParams(vmem_limit_bytes=50*2**20),
    )(shift, band, coefs, observed, inv_var, fwd, adj)


E_AXIS, P_AXIS = "exp", "pix"
MESH_ID = pl.DeviceIdType.MESH
GROUPS = ((0, 1), (2, 3))


def greet(me_e, me_p, ne, np_):
    barrier = pltpu.get_barrier_semaphore()
    for d in range(1, ne):
        pl.semaphore_signal(barrier, inc=1, device_id=(lax.rem(me_e + d, ne), me_p), device_id_type=MESH_ID)
    for d in range(1, np_):
        pl.semaphore_signal(barrier, inc=1, device_id=(me_e, lax.rem(me_p + d, np_)), device_id_type=MESH_ID)
    return lambda: pl.semaphore_wait(barrier, ne + np_ - 2)


def remote(src, dst, send, recv, device):
    return pltpu.make_async_remote_copy(
        src_ref=src, dst_ref=dst, send_sem=send, recv_sem=recv, device_id=device, device_id_type=MESH_ID
    )


def row_base(offs_ref, exposure, strip):
    phase = offs_ref[exposure, 0] >> 5
    return phase, jnp.where(strip < phase, 4, 0)


def gather_kernel(foot, offs, slots, sky, band, *scratch):
    ng = len(GROUPS)
    recv1, recv2 = scratch[0:ng], scratch[ng:2 * ng]
    stage1, stage2, stage3, s1, r1, s2, r2, s3, r3 = scratch[2 * ng:]
    ne, np_ = 8, 16
    me_e, me_p = lax.axis_index(E_AXIS), lax.axis_index(P_AXIS)
    arrived = greet(me_e, me_p, ne, np_)

    def fill(g, carry):
        for q in range(4):
            _, base = row_base(offs, 4 * g + q, me_p)
            local = jnp.int32(0)
            for j in range(4):
                slot = slots[foot[4 * g + q, base + j]]
                local = jnp.where((slot >> 6) == me_e, slot & 63, local)
            stage1[g, q] = sky[local]
        return carry

    lax.fori_loop(0, ne, fill, 0)
    arrived()
    first, second, third = [], [], []
    for n, group in enumerate(GROUPS):
        q0, nq = group[0], len(group)
        copies = []
        for d in range(1, ne):
            g = lax.rem(me_e + d, ne)
            o = lax.rem(me_e + ne - d, ne)
            out = remote(stage1.at[g, pl.ds(q0, nq)], recv1[n].at[me_e], s1.at[n, g], r1.at[n, me_e], (g, me_p))
            out.start()
            copies.append((out, remote(stage1.at[g, pl.ds(q0, nq)], recv1[n].at[o], s1.at[n, g], r1.at[n, o], (g, me_p))))
        recv1[n][me_e] = stage1[me_e, q0:q0 + nq]
        first.append(copies)
    for n, group in enumerate(GROUPS):
        q0, nq = group[0], len(group)
        for _, inward in first[n]:
            inward.wait_recv()
        for k, q in enumerate(group):
            e = 4 * me_e + q
            _, base = row_base(offs, e, me_p)
            for j in range(4):
                source = slots[foot[e, base + j]] >> 6
                tile = recv1[n][source, k]
                for c in range(4):
                    stage2[4 * j + c, q] = tile[:, c * 128:(c + 1) * 128]
        copies = []
        for d in range(1, np_):
            i = lax.rem(me_p + d, np_)
            o = lax.rem(me_p + np_ - d, np_)
            src = stage2.at[i, pl.ds(q0, nq)]
            out = remote(src, recv2[n].at[me_p], s2.at[n, i], r2.at[n, me_p], (me_e, i))
            out.start()
            copies.append((out, remote(src, recv2[n].at[o], s2.at[n, i], r2.at[n, o], (me_e, i))))
        recv2[n][me_p] = stage2[me_p, q0:q0 + nq]
        second.append(copies)
    mine = pl.ds(pl.multiple_of(me_p * 128, 128), 128)
    for n, group in enumerate(GROUPS):
        q0, nq = group[0], len(group)
        for _, inward in second[n]:
            inward.wait_recv()
        for k, q in enumerate(group):
            phase = offs[4 * me_e + q, 0] >> 5
            for to in range(np_):
                strip = (phase + to) & 15
                stage3[to, q, 16:48] = recv2[n][strip, k]
                if to > 0:
                    stage3[to, q, 0:16] = recv2[n][(strip + 15) & 15, k, 16:32]
                else:
                    stage3[to, q, 0:16] = jnp.zeros((16, 128), jnp.bfloat16)
                if to < np_ - 1:
                    stage3[to, q, 48:64] = recv2[n][(strip + 1) & 15, k, 0:16]
                else:
                    stage3[to, q, 48:64] = jnp.zeros((16, 128), jnp.bfloat16)
        copies = []
        for d in range(1, np_):
            i = lax.rem(me_p + d, np_)
            o = lax.rem(me_p + np_ - d, np_)
            theirs = pl.ds(pl.multiple_of(o * 128, 128), 128)
            src = stage3.at[i, pl.ds(q0, nq)]
            out = remote(src, band.at[pl.ds(q0, nq), :, mine], s3.at[n, i], r3.at[n, me_p], (me_e, i))
            out.start()
            copies.append((out, remote(src, band.at[pl.ds(q0, nq), :, theirs], s3.at[n, i], r3.at[n, o], (me_e, i))))
        band[q0:q0 + nq, :, mine] = stage3[me_p, q0:q0 + nq]
        third.append(copies)
    for copies in third:
        for _, inward in copies:
            inward.wait_recv()
    for copies in first + second + third:
        for out, _ in copies:
            out.wait_send()


def gather_bands(footprints, offsets, tile_slot, sky):
    ng = len(GROUPS)
    bf = jnp.bfloat16
    dma = pltpu.SemaphoreType.DMA
    smem = pl.BlockSpec(memory_space=pltpu.SMEM)
    vmem = pl.BlockSpec(memory_space=pltpu.VMEM)
    return pl.pallas_call(
        gather_kernel,
        out_shape=jax.ShapeDtypeStruct((4, 64, 2048), bf),
        in_specs=[smem, smem, smem, vmem],
        out_specs=vmem,
        scratch_shapes=[pltpu.VMEM((8, len(g), 32, 512), bf) for g in GROUPS]
        + [pltpu.VMEM((16, len(g), 32, 128), bf) for g in GROUPS]
        + [pltpu.VMEM((8, 4, 32, 512), bf), pltpu.VMEM((16, 4, 32, 128), bf), pltpu.VMEM((16, 4, 64, 128), bf)]
        + [dma((ng, 8)), dma((ng, 8))] + [dma((ng, 16))] * 4,
        compiler_params=pltpu.CompilerParams(collective_id=0, has_side_effects=True, vmem_limit_bytes=40 * 2**20),
        name="gather_bands",
    )(footprints, offsets, tile_slot, sky)


def scatter_kernel(foot, offs, slots, back, pieces, *scratch):
    ng = len(GROUPS)
    recv1, recv2 = scratch[0:ng], scratch[ng:2 * ng]
    stage2, stage3, s1, r1, s2, r2, s3, r3 = scratch[2 * ng:]
    ne, np_ = 8, 16
    me_e, me_p = lax.axis_index(E_AXIS), lax.axis_index(P_AXIS)
    greet(me_e, me_p, ne, np_)()
    mine = pl.ds(pl.multiple_of(me_p * 128, 128), 128)
    first, second, third = [], [], []
    for n, group in enumerate(GROUPS):
        q0, nq = group[0], len(group)
        copies = []
        for d in range(1, np_):
            i = lax.rem(me_p + d, np_)
            o = lax.rem(me_p + np_ - d, np_)
            src = back.at[pl.ds(q0, nq), :, pl.ds(pl.multiple_of(i * 128, 128), 128)]
            out = remote(src, recv1[n].at[me_p], s1.at[n, i], r1.at[n, me_p], (me_e, i))
            out.start()
            copies.append((out, remote(src, recv1[n].at[o], s1.at[n, i], r1.at[n, o], (me_e, i))))
        recv1[n][me_p] = back[q0:q0 + nq, :, mine]
        first.append(copies)
    for n, group in enumerate(GROUPS):
        q0, nq = group[0], len(group)
        for _, inward in first[n]:
            inward.wait_recv()
        for k, q in enumerate(group):
            phase = offs[4 * me_e + q, 0] >> 5
            for to in range(np_):
                strip = (to - phase) & 15
                centre = recv1[n][strip, k, 16:48].astype(jnp.float32)
                above = recv1[n][(strip + 15) & 15, k, 48:64].astype(jnp.float32)
                below = recv1[n][(strip + 1) & 15, k, 0:16].astype(jnp.float32)
                above = jnp.where(strip > 0, above, 0.0)
                below = jnp.where(strip < np_ - 1, below, 0.0)
                stage2[to, q, 0:16] = (centre[0:16] + above).astype(jnp.bfloat16)
                stage2[to, q, 16:32] = (centre[16:32] + below).astype(jnp.bfloat16)
        copies = []
        for d in range(1, np_):
            i = lax.rem(me_p + d, np_)
            o = lax.rem(me_p + np_ - d, np_)
            src = stage2.at[i, pl.ds(q0, nq)]
            out = remote(src, recv2[n].at[me_p], s2.at[n, i], r2.at[n, me_p], (me_e, i))
            out.start()
            copies.append((out, remote(src, recv2[n].at[o], s2.at[n, i], r2.at[n, o], (me_e, i))))
        recv2[n][me_p] = stage2[me_p, q0:q0 + nq]
        second.append(copies)
    for n, group in enumerate(GROUPS):
        q0, nq = group[0], len(group)
        for _, inward in second[n]:
            inward.wait_recv()
        for k, q in enumerate(group):
            e = 4 * me_e + q
            _, base = row_base(offs, e, me_p)
            source = [slots[foot[e, base + j]] >> 6 for j in range(4)]
            for o in range(ne):
                which = jnp.int32(0)
                for j in range(1, 4):
                    which = jnp.where(source[j] == o, j, which)
                for c in range(4):
                    stage3[o, q, :, c * 128:(c + 1) * 128] = recv2[n][4 * which + c, k]
        copies = []
        for d in range(1, ne):
            g = lax.rem(me_e + d, ne)
            o = lax.rem(me_e + ne - d, ne)
            src = stage3.at[g, pl.ds(q0, nq)]
            out = remote(src, pieces.at[me_e, pl.ds(q0, nq)], s3.at[n, g], r3.at[n, me_e], (g, me_p))
            out.start()
            copies.append((out, remote(src, pieces.at[o, pl.ds(q0, nq)], s3.at[n, g], r3.at[n, o], (g, me_p))))
        pieces[me_e, q0:q0 + nq] = stage3[me_e, q0:q0 + nq]
        third.append(copies)
    for copies in third:
        for _, inward in copies:
            inward.wait_recv()
    for copies in first + second + third:
        for out, _ in copies:
            out.wait_send()


def scatter_pieces(footprints, offsets, tile_slot, back):
    ng = len(GROUPS)
    bf = jnp.bfloat16
    dma = pltpu.SemaphoreType.DMA
    smem = pl.BlockSpec(memory_space=pltpu.SMEM)
    vmem = pl.BlockSpec(memory_space=pltpu.VMEM)
    return pl.pallas_call(
        scatter_kernel,
        out_shape=jax.ShapeDtypeStruct((8, 4, 32, 512), bf),
        in_specs=[smem, smem, smem, vmem],
        out_specs=vmem,
        scratch_shapes=[pltpu.VMEM((16, len(g), 64, 128), bf) for g in GROUPS]
        + [pltpu.VMEM((16, len(g), 32, 128), bf) for g in GROUPS]
        + [pltpu.VMEM((16, 4, 32, 128), bf), pltpu.VMEM((8, 4, 32, 512), bf)]
        + [dma((ng, 16))] * 4 + [dma((ng, 8)), dma((ng, 8))],
        compiler_params=pltpu.CompilerParams(collective_id=1, has_side_effects=True, vmem_limit_bytes=40 * 2**20),
        name="scatter_pieces",
    )(footprints, offsets, tile_slot, back)


def total_kernel(foot, offs, slots, pieces, out):
    me_e, me_p = lax.axis_index(E_AXIS), lax.axis_index(P_AXIS)

    def clear(r, carry):
        out[r] = jnp.zeros(out.shape[1:], jnp.float32)
        return carry

    lax.fori_loop(0, out.shape[0], clear, 0)

    def add(g, carry):
        for q in range(4):
            _, base = row_base(offs, 4 * g + q, me_p)
            local, held = jnp.int32(0), jnp.int32(0)
            for j in range(4):
                slot = slots[foot[4 * g + q, base + j]]
                local = jnp.where((slot >> 6) == me_e, slot & 63, local)
                held = jnp.where((slot >> 6) == me_e, 1, held)

            @pl.when(held == 1)
            def _():
                out[local] = out[local] + pieces[g, q].astype(jnp.float32)
        return carry

    lax.fori_loop(0, 8, add, 0)


def total(footprints, offsets, tile_slot, pieces):
    smem = pl.BlockSpec(memory_space=pltpu.SMEM)
    vmem = pl.BlockSpec(memory_space=pltpu.VMEM)
    return pl.pallas_call(
        total_kernel,
        out_shape=jax.ShapeDtypeStruct((64, 32, 512), jnp.float32),
        in_specs=[smem, smem, smem, vmem],
        out_specs=vmem,
        compiler_params=pltpu.CompilerParams(vmem_limit_bytes=40 * 2**20),
        name="total",
    )(footprints, offsets, tile_slot, pieces)


def local(sky, kernels, coefs, observed, inv_var, footprints, offsets, tile_slot):
    shift = lax.dynamic_slice_in_dim(offsets[:, 1], 4 * lax.axis_index(E_AXIS), 4) - 12
    fwd, adj = tables(kernels)
    band = gather_bands(footprints, offsets, tile_slot, sky)
    back = blur(shift, band, coefs, observed, inv_var, fwd, adj, jnp.bfloat16)
    pieces = scatter_pieces(footprints, offsets, tile_slot, back)
    return total(footprints, offsets, tile_slot, pieces)


def solution(mesh):
    return jax.shard_map(
        local,
        mesh=mesh,
        in_specs=(
            P("exp", "pix", None),
            P(),
            P("exp", None, "pix", None),
            P("exp", "pix", None),
            P("exp", "pix", None),
            P(),
            P(),
            P(),
        ),
        out_specs=P("exp", "pix", None),
        check_vma=False,
    )
```

time: 203 us -> 117 us (0.58)
  Pallas kernels: 18 us -> 101 us
  waiting for transfers between devices: 81.9 us -> 0 us
  starting transfers between devices: 42.6 us -> 0 us
  other arithmetic: 22.7 us -> 0.09 us
  local copies, waits for them, and re-layouts: 33.7 us -> 15.1 us
    pallas_call x0 -> x3, Pallas kernels: none -> 83.7 us  [the longest x1 40.9 us: gather_bands(): pl.pallas_call(gather_kernel, out_shape=jax.ShapeDtypeStruct((4, 64, 2048...]
    all_to_all x4 -> x0, waiting for transfers between devices: 76.1 us -> none  [the longest x1 24.6 us: local(): lax.all_to_all(forward_rows, 'pix', split_axis=0, concat_axis=0, tiled=True)]
    all_to_all x4 -> x0, starting transfers between devices: 33.2 us -> none  [the longest x1 9.89 us: local(): lax.all_to_all(to_owners, 'exp', split_axis=0, concat_axis=0, tiled=True)]
    gather x17 -> x0, local copies, waits for them, and re-layouts: 14.8 us -> none  [the longest x1 2.17 us: local(): mine = landed[(my_phase + strip_index) % strip_count]]
    select_n x16 -> x0, other arithmetic: 9.68 us -> none  [the longest x1 3.12 us: local(): jnp.where(back_has[:, None, None, None], pieces[back_visit], nothing)]
    ppermute x4 -> x0, starting transfers between devices: 9.47 us -> none  [the longest x2 5.29 us: passed_along(): return lax.ppermute(x, axis, pairs)]
    scatter-add x1 -> x0, other arithmetic: 6.95 us -> none  [local(): gradient.at[held_rows.reshape(-1)]]
    ppermute x4 -> x0, waiting for transfers between devices: 5.71 us -> none  [the longest x2 5.7 us: passed_along(): return lax.ppermute(x, axis, pairs)]
  transfers between devices with their start and end apart: 8 -> 0, of which waited for: 6 -> 0; matrix products, arithmetic and copies ran while one was open for 8% -> 0% of each run, Pallas kernels for 0% -> 0%
where the time goes in v2:
time: 117 us
  Pallas kernels  101 us (86%)
  local copies, waits for them, and re-layouts  15.1 us (13%)
    pallas_call x1, Pallas kernels, gather_bands(): pl.pallas_call(gather_kernel, out_shape=jax.ShapeDtypeStruct((4, 64, 2048...  40.9 us
    pallas_call x1, Pallas kernels, scatter_pieces(): pl.pallas_call(scatter_kernel, out_shape=jax.ShapeDtypeStruct((8, 4, 32,...  38.3 us
    pallas_call x1, Pallas kernels, blur(): pl.pallas_call(blur_kernel, grid_spec=pltpu.PrefetchScalarGridSpec(num_sc...  17.2 us
    unnamed x16, local copies, waits for them, and re-layouts  4.78 us
    pallas_call x1, Pallas kernels, total(): pl.pallas_call(total_kernel, out_shape=jax.ShapeDtypeStruct((64, 32, 512)...  4.5 us
    reshape x2, local copies, waits for them, and re-layouts, tables(): t.reshape(nb, 5, 5, tall, rows).transpose(1, 3, 2, 0, 4)  3.18 us

profile of v2, /device:TPU:1, one launch (start us, length us, event | category | flops | bytes accessed | tf_op | source)
XLA Modules:
  0.0 116.7 jit_solution(3744355047926373459)
XLA Ops:
  0.0 0.0 copy-start
  0.0 0.8 copy.27.foot
  0.8 0.8 copy.28.offs
  1.5 0.7 slice.3
  2.2 0.1 add_bitcast_fusion.shift_ref
  2.3 0.0 copy-start.2
  2.3 1.6 %copy-done.2 = bf16[64,32,512]{2,1,0:T(8,128)(2,1)S(1)} copy-done((bf16[64,32,512]{2,1,0:T(8,128)(2,1)S(1)}, bf16[64,32,512]{2,1,0:T(8,128)(2,1)}, u32[]{:S(2)}) %copy-start.2) | copy-done | bytes 2097176
  3.9 0.0 copy-start.5
  3.9 0.7 copy-done.5
  4.6 40.9 %gather_bands.1.band_ref = bf16[4,64,2048]{2,1,0:T(8,128)(2,1)S(1)} custom-call(s32[32,8]{1,0:T(8,128)S(1)} %copy.27.foot, s32[32,2]{1,0:T(8,128)S(1)} %copy.28.offs, s32[512]{0:T(512)S(1)} %copy-done.5, bf16[64,32,512]{2,1,0:T(8,128)(2,1)S(1)} %copy-done.2), custom_call_target="tpu_custom_call" | custom-call | tf_op jit(solution)/shard_map/gather_bands/pallas_call | solution.py:188
  45.5 0.0 copy-start.1
  45.5 1.0 copy-done.1
  46.4 0.0 copy-done
  46.4 0.6 convolution_convert_fusion
  47.1 1.4 %copy.21 = bf16[6,32,25,64]{3,2,1,0:T(8,128)(2,1)} copy(bf16[6,32,25,64]{3,2,0,1:T(8,128)(2,1)S(1)} %bitcast.17) | data formatting | bytes 1228800 | tf_op jit(solution)/shard_map/convert_element_type | solution.py:14
  48.5 2.3 %reshape.40.fwd_ref = bf16[192,1600]{1,0:T(8,128)(2,1)S(1)} reshape(bf16[6,32,25,64]{3,2,1,0:T(8,128)(2,1)} %copy.21) | data formatting | bytes 1228800 | tf_op jit(solution)/shard_map/reshape | solution.py:15
  50.8 0.8 copy.22
  51.6 1.9 %copy.23 = bf16[5,64,5,6,32]{1,0,4,3,2:T(8,128)(2,1)} copy(bf16[5,64,5,6,32]{1,4,2,0,3:T(8,128)(2,1)S(1)} %bitcast.19) | data formatting | bytes 1228800 | tf_op jit(solution)/shard_map/transpose | solution.py:16
  53.5 0.0 copy-start.3
  53.5 0.0 copy-start.4
  53.5 2.9 %reshape.42 = bf16[320,960]{0,1:T(8,128)(2,1)S(1)} reshape(bf16[5,64,5,6,32]{1,0,4,3,2:T(8,128)(2,1)} %copy.23) | data formatting | bytes 1228800 | tf_op jit(solution)/shard_map/reshape | solution.py:16
  56.4 0.3 copy.24.adj_ref
  56.7 0.0 copy-done.3
  56.7 0.0 copy-done.4
  56.7 0.0 copy-start.6
  56.7 17.2 %shard_map.82.back = bf16[4,64,2048]{2,1,0:T(8,128)(2,1)S(1)} custom-call(s32[4]{0:T(128)S(1)} %add_bitcast_fusion.shift_ref, bf16[4,64,2048]{2,1,0:T(8,128)(2,1)} %copy-done.1, bf16[4,6,32,1536]{3,2,1,0:T(8,128)(2,1)} %coef_ref.1, f32[4,32,1536]{2,1,0:T(8,128)S(1)} %copy-done.3, bf16[4,32,1536]{2,1,0:T(8,128)(2,1)S(1)} %copy-done.4, ...), custom_call_target="tpu_custom_call" | custom-call | tf_op jit(solution)/shard_map/pallas_call | solution.py:54
  73.9 0.0 copy-done.6
  73.9 38.3 %scatter_pieces.1.pieces = bf16[8,4,32,512]{3,2,1,0:T(8,128)(2,1)S(1)} custom-call(s32[32,8]{1,0:T(8,128)S(1)} %copy.27.foot, s32[32,2]{1,0:T(8,128)S(1)} %copy.28.offs, s32[512]{0:T(512)S(1)} %copy-done.6, bf16[4,64,2048]{2,1,0:T(8,128)(2,1)S(1)} %shard_map.82.back), custom_call_target="tpu_custom_call" | custom-call | tf_op jit(solution)/shard_map/scatter_pieces/pallas_call | solution.py:286
  112.2 4.5 %total.1 = f32[64,32,512]{2,1,0:T(8,128)} custom-call(s32[32,8]{1,0:T(8,128)S(1)} %copy.27.foot, s32[32,2]{1,0:T(8,128)S(1)} %copy.28.offs, s32[512]{0:T(512)S(1)} %copy-done.6, bf16[8,4,32,512]{3,2,1,0:T(8,128)(2,1)S(1)} %scatter_pieces.1.pieces), custom_call_target="tpu_custom_call" | custom-call | tf_op jit(solution)/shard_map/total/pallas_call | solution.py:329
  (2 shorter events, 0.0 us)
Async XLA Ops:
  0.0 46.4 %copy-start = (bf16[6,25,25]{2,1,0:T(8,128)(2,1)S(1)}, bf16[6,25,25]{2,1,0:T(8,128)(2,1)}, u32[]{:S(2)}) copy-start(bf16[6,25,25]{2,1,0:T(8,128)(2,1)} %param.9) | copy-start | bytes 22504
  2.3 1.6 %copy-start.2 = (bf16[64,32,512]{2,1,0:T(8,128)(2,1)S(1)}, bf16[64,32,512]{2,1,0:T(8,128)(2,1)}, u32[]{:S(2)}) copy-start(bf16[64,32,512]{2,1,0:T(8,128)(2,1)} %sky.1) | copy-start | bytes 6291460
  3.9 0.7 copy-start.5
  45.5 1.0 copy-start.1
  53.5 3.2 %copy-start.3 = (f32[4,32,1536]{2,1,0:T(8,128)S(1)}, f32[4,32,1536]{2,1,0:T(8,128)}, u32[]{:S(2)}) copy-start(f32[4,32,1536]{2,1,0:T(8,128)} %obs_ref.1) | copy-start | bytes 2359300
  53.5 3.2 %copy-start.4 = (bf16[4,32,1536]{2,1,0:T(8,128)(2,1)S(1)}, bf16[4,32,1536]{2,1,0:T(8,128)(2,1)}, u32[]{:S(2)}) copy-start(bf16[4,32,1536]{2,1,0:T(8,128)(2,1)} %inv_ref.1) | copy-start | bytes 1179652
  56.7 17.2 %copy-start.6 = (s32[512]{0:T(512)S(1)}, s32[512]{0:T(512)}, u32[]{:S(2)}) copy-start(s32[512]{0:T(512)} %slots.5) | copy-start | bytes 6148

commit v3 on v1

v3 whole, which is shorter than its diff:
```python
import jax
import jax.numpy as jnp
from jax import lax
from jax.experimental import pallas as pl
from jax.experimental.pallas import tpu as pltpu
from jax.sharding import PartitionSpec as P

E_AXIS, P_AXIS = "exp", "pix"
MESH_ID = pl.DeviceIdType.MESH
KS, NB, RIM, NV = 25, 6, 12, 4
NE, NP = 8, 16
ROWS, TALL, LANES = 32, 64, 128
WIDTH, SPAN, FULL = 1536, 1664, 2048
BF, F32 = jnp.bfloat16, jnp.float32


def tables_kernel(kt, fwd, adj):
    lane = lax.broadcasted_iota(jnp.int32, (ROWS, LANES), 1)
    tail = {}
    for m in range(13):
        blocks = []
        for b in range(NB):
            low = pltpu.roll(jnp.broadcast_to(kt[b, 2 * m:2 * m + 1, :], (ROWS, LANES)), 0, axis=1, stride=1, stride_axis=0)
            if 2 * m + 1 < KS:
                high = pltpu.roll(
                    jnp.broadcast_to(kt[b, 2 * m + 1:2 * m + 2, :], (ROWS, LANES)), TALL, axis=1, stride=1, stride_axis=0
                )
                block = jnp.where(lane < TALL, low, high)
                fwd[b * ROWS:(b + 1) * ROWS, m * LANES:(m + 1) * LANES] = block.astype(BF)
            else:
                block = low
                fwd[b * ROWS:(b + 1) * ROWS, m * LANES:m * LANES + TALL] = block[:, :TALL].astype(BF)
            blocks.append(block)
        turned_a = jnp.concatenate(blocks[:4], axis=0).T
        turned_b = jnp.concatenate(blocks[4:] + [jnp.zeros((2 * ROWS, LANES), F32)], axis=0).T
        for h in range(2):
            v = 2 * m + h
            if v < KS:
                a, c = divmod(v, 5)
                adj[a * TALL:(a + 1) * TALL, c * LANES:(c + 1) * LANES] = turned_a[h * TALL:(h + 1) * TALL].astype(BF)
                tail[a, c] = turned_b[h * TALL:(h + 1) * TALL]
    wide_lane = lax.broadcasted_iota(jnp.int32, (TALL, LANES), 1)
    for a in range(5):
        for c in (0, 2):
            pair = jnp.where(wide_lane < 64, tail[a, c], pltpu.roll(tail[a, c + 1], 64, axis=1))
            adj[a * TALL:(a + 1) * TALL, 640 + c * 64:640 + c * 64 + LANES] = pair.astype(BF)
        adj[a * TALL:(a + 1) * TALL, 896:960] = tail[a, 4][:, :64].astype(BF)


def tables(kernels):
    kt = jnp.pad(kernels.transpose(0, 2, 1).astype(F32), ((0, 0), (0, 0), (4, LANES - KS - 4)))
    vmem = pl.BlockSpec(memory_space=pltpu.VMEM)
    return pl.pallas_call(
        tables_kernel,
        out_shape=(jax.ShapeDtypeStruct((NB * ROWS, KS * TALL), BF), jax.ShapeDtypeStruct((5 * TALL, 5 * NB * ROWS), BF)),
        in_specs=[vmem],
        out_specs=(vmem, vmem),
        compiler_params=pltpu.CompilerParams(vmem_limit_bytes=30 * 2**20),
        name="tables",
    )(kt)


def blur_step(q, shift, band, coef_ref, obs_ref, inv_ref, fwd, adj, stack, wide, back_ref):
    win = pltpu.roll(band[q].astype(F32), (FULL - shift) & (FULL - 1), axis=1)[:, :SPAN].astype(BF)
    for v in range(KS):
        stack[v * TALL:(v + 1) * TALL, :] = win[:, v:v + WIDTH]
    nc = 512
    wide[0:128, WIDTH:] = jnp.zeros((128, SPAN - WIDTH), BF)
    wide[640:704, WIDTH:] = jnp.zeros((64, SPAN - WIDTH), BF)

    def chunk(n, carry):
        cols = pl.ds(pl.multiple_of(n * nc, nc), nc)
        blurred = jnp.dot(fwd[...], stack[:, cols], preferred_element_type=F32)
        coef = [coef_ref[q, b, :, cols].astype(F32) for b in range(NB)]
        model = coef[0] * blurred[0:ROWS]
        for b in range(1, NB):
            model = model + coef[b] * blurred[b * ROWS:(b + 1) * ROWS]
        resid = inv_ref[q, :, cols].astype(F32) * (model - obs_ref[q, :, cols])
        for b in range(NB):
            at = b * ROWS if b < 4 else 640 + (b - 4) * ROWS
            wide[at:at + ROWS, cols] = (coef[b] * resid).astype(BF)
        return carry

    lax.fori_loop(0, WIDTH // nc, chunk, 0)
    head, rest = wide[0:128, :], wide[640:704, :]
    for c in range(1, 5):
        wide[c * 128:(c + 1) * 128, :] = jnp.concatenate([jnp.zeros((128, c), BF), head[:, :SPAN - c]], axis=1)
        wide[640 + c * 64:640 + (c + 1) * 64, :] = jnp.concatenate([jnp.zeros((64, c), BF), rest[:, :SPAN - c]], axis=1)
    part = jnp.dot(adj[...], wide[...], preferred_element_type=F32)
    back = part[0:TALL]
    for a in range(1, 5):
        back = back + pltpu.roll(part[a * TALL:(a + 1) * TALL], 5 * a, axis=1)
    back = jnp.concatenate([back, jnp.zeros((TALL, FULL - SPAN), F32)], axis=1)
    back_ref[q] = pltpu.roll(back, shift, axis=1).astype(BF)


def fused_kernel(foot, offs, slots, sky_hbm, coefs_hbm, obs_hbm, inv_hbm, fwd, adj, pieces, *scratch):
    recv1, recv2, recv4, recv5 = (scratch[4 * k:4 * k + 4] for k in range(4))
    (sky, coef, obs, inv, stage1, stage2, stage3, stage5, stage6, band, back, stack, wide,
     s1, r1, s2, r2, s3, r3, s4, r4, s5, r5, s6, r6, loads) = scratch[16:]
    me_e, me_p = lax.axis_index(E_AXIS), lax.axis_index(P_AXIS)
    barrier = pltpu.get_barrier_semaphore()
    for d in range(1, NE):
        pl.semaphore_signal(barrier, inc=1, device_id=(lax.rem(me_e + d, NE), me_p), device_id_type=MESH_ID)
    for d in range(1, NP):
        pl.semaphore_signal(barrier, inc=1, device_id=(me_e, lax.rem(me_p + d, NP)), device_id_type=MESH_ID)
    sky_load = pltpu.make_async_copy(sky_hbm, sky, loads.at[0])
    sky_load.start()
    rest_loads = [
        pltpu.make_async_copy(src, dst, loads.at[k])
        for k, (src, dst) in enumerate(((coefs_hbm, coef), (obs_hbm, obs), (inv_hbm, inv)), 1)
    ]
    for load in rest_loads:
        load.start()
    sky_load.wait()

    def base_of(exposure):
        return jnp.where(me_p < (offs[exposure, 0] >> 5), 4, 0)

    def fill(g, carry):
        for q in range(NV):
            base = base_of(4 * g + q)
            local = jnp.int32(0)
            for j in range(4):
                slot = slots[foot[4 * g + q, base + j]]
                local = jnp.where((slot >> 6) == me_e, slot & 63, local)
            stage1[g, q] = sky[local]
        return carry

    lax.fori_loop(0, NE, fill, 0)
    phase = [offs[4 * me_e + q, 0] >> 5 for q in range(NV)]
    shift = [offs[4 * me_e + q, 1] - RIM for q in range(NV)]
    source = []
    for q in range(NV):
        base = base_of(4 * me_e + q)
        source.append([slots[foot[4 * me_e + q, base + j]] >> 6 for j in range(4)])
    pl.semaphore_wait(barrier, NE + NP - 2)

    sent = []

    def exchange(count, me, device, src, dst, send, recv):
        inward = []
        for d in range(1, count):
            to, of = lax.rem(me + d, count), lax.rem(me + count - d, count)
            make = lambda slot, sem: pltpu.make_async_remote_copy(
                src_ref=src(to), dst_ref=dst(slot), send_sem=send.at[to], recv_sem=recv.at[sem],
                device_id=device(to), device_id_type=MESH_ID)
            out = make(me, me)
            out.start()
            sent.append(out)
            inward.append(make(of, of))
        return inward

    over_e, over_p = (lambda to: (to, me_p)), (lambda to: (me_e, to))

    def lanes(i):
        return pl.ds(pl.multiple_of(i * LANES, LANES), LANES)

    def arrive(copies):
        for copy in copies:
            copy.wait_recv()

    def step1(q):
        recv1[q][me_e] = stage1[me_e, q]
        return exchange(NE, me_e, over_e, lambda to: stage1.at[to, q], lambda i: recv1[q].at[i], s1.at[q], r1.at[q])

    def step2(q):
        for j in range(4):
            tile = recv1[q][source[q][j]]
            for c in range(4):
                stage2[4 * j + c, q] = tile[:, c * LANES:(c + 1) * LANES]
        recv2[q][me_p] = stage2[me_p, q]
        return exchange(NP, me_p, over_p, lambda to: stage2.at[to, q], lambda i: recv2[q].at[i], s2.at[q], r2.at[q])

    def step3(q):
        for to in range(NP):
            strip = (phase[q] + to) & 15
            stage3[to, q, 16:48] = recv2[q][strip]
            if to > 0:
                stage3[to, q, 0:16] = recv2[q][(strip + 15) & 15, 16:32]
            else:
                stage3[to, q, 0:16] = jnp.zeros((16, LANES), BF)
            if to < NP - 1:
                stage3[to, q, 48:64] = recv2[q][(strip + 1) & 15, 0:16]
            else:
                stage3[to, q, 48:64] = jnp.zeros((16, LANES), BF)
        band[q, :, lanes(me_p)] = stage3[me_p, q]
        return exchange(NP, me_p, over_p, lambda to: stage3.at[to, q], lambda i: band.at[q, :, lanes(i)], s3.at[q], r3.at[q])

    def step4(q):
        blur_step(q, shift[q], band, coef, obs, inv, fwd, adj, stack, wide, back)
        recv4[q][me_p] = back[q, :, lanes(me_p)]
        return exchange(NP, me_p, over_p, lambda to: back.at[q, :, lanes(to)], lambda i: recv4[q].at[i], s4.at[q], r4.at[q])

    def step5(q):
        for to in range(NP):
            strip = (to - phase[q]) & 15
            centre = recv4[q][strip, 16:48].astype(F32)
            above = jnp.where(strip > 0, recv4[q][(strip + 15) & 15, 48:64].astype(F32), 0.0)
            below = jnp.where(strip < NP - 1, recv4[q][(strip + 1) & 15, 0:16].astype(F32), 0.0)
            stage5[to, q, 0:16] = (centre[0:16] + above).astype(BF)
            stage5[to, q, 16:32] = (centre[16:32] + below).astype(BF)
        recv5[q][me_p] = stage5[me_p, q]
        return exchange(NP, me_p, over_p, lambda to: stage5.at[to, q], lambda i: recv5[q].at[i], s5.at[q], r5.at[q])

    def step6(q):
        for o in range(NE):
            which = jnp.int32(0)
            for j in range(1, 4):
                which = jnp.where(source[q][j] == o, j, which)
            for c in range(4):
                stage6[o, q, :, c * LANES:(c + 1) * LANES] = recv5[q][4 * which + c]
        pieces[me_e, q] = stage6[me_e, q]
        return exchange(NE, me_e, over_e, lambda to: stage6.at[to, q], lambda i: pieces.at[i, q], s6.at[q], r6.at[q])

    steps = (step1, step2, step3, step4, step5, step6)
    order = ORDER
    waiting = {}
    loaded = False
    for n, q in order:
        if n > 1:
            arrive(waiting.pop((n - 1, q)))
        if n == 4 and not loaded:
            for load in rest_loads:
                load.wait()
            loaded = True
        waiting[n, q] = steps[n - 1](q)
    for q in range(NV):
        arrive(waiting.pop((6, q)))
    for out in sent:
        out.wait_send()


ORDER = (
    (1, 0), (1, 1), (1, 2), (1, 3), (2, 0), (2, 1), (3, 0), (2, 2), (3, 1), (2, 3), (3, 2), (4, 0), (3, 3), (4, 1), (5, 0),
    (4, 2), (5, 1), (6, 0), (4, 3), (5, 2), (6, 1), (5, 3), (6, 2), (6, 3),
)


def fused(footprints, offsets, tile_slot, sky, coefs, observed, inv_var, fwd, adj):
    dma = pltpu.SemaphoreType.DMA
    smem = pl.BlockSpec(memory_space=pltpu.SMEM)
    vmem = pl.BlockSpec(memory_space=pltpu.VMEM)
    hbm = pl.BlockSpec(memory_space=pl.ANY)
    shapes = [(NE, ROWS, 512)] * 4 + [(NP, ROWS, LANES)] * 4 + [(NP, TALL, LANES)] * 4 + [(NP, ROWS, LANES)] * 4
    return pl.pallas_call(
        fused_kernel,
        out_shape=jax.ShapeDtypeStruct((NE, NV, ROWS, 512), BF),
        in_specs=[smem, smem, smem, hbm, hbm, hbm, hbm, vmem, vmem],
        out_specs=vmem,
        scratch_shapes=[pltpu.VMEM(s, BF) for s in shapes]
        + [
            pltpu.VMEM(sky.shape, BF),
            pltpu.VMEM(coefs.shape, BF),
            pltpu.VMEM(observed.shape, F32),
            pltpu.VMEM(inv_var.shape, BF),
            pltpu.VMEM((NE, NV, ROWS, 512), BF),
            pltpu.VMEM((NP, NV, ROWS, LANES), BF),
            pltpu.VMEM((NP, NV, TALL, LANES), BF),
            pltpu.VMEM((NP, NV, ROWS, LANES), BF),
            pltpu.VMEM((NE, NV, ROWS, 512), BF),
            pltpu.VMEM((NV, TALL, FULL), BF),
            pltpu.VMEM((NV, TALL, FULL), BF),
            pltpu.VMEM((KS * TALL, WIDTH), BF),
            pltpu.VMEM((5 * NB * ROWS, SPAN), BF),
        ]
        + [dma((NV, NE))] * 2 + [dma((NV, NP))] * 8 + [dma((NV, NE))] * 2 + [dma((4,))],
        compiler_params=pltpu.CompilerParams(collective_id=0, has_side_effects=True, vmem_limit_bytes=50 * 2**20),
        name="fused",
    )(footprints, offsets, tile_slot, sky, coefs, observed, inv_var, fwd, adj)


def total_kernel(foot, offs, slots, pieces, out):
    me_e, me_p = lax.axis_index(E_AXIS), lax.axis_index(P_AXIS)

    def clear(r, carry):
        out[r] = jnp.zeros(out.shape[1:], F32)
        return carry

    lax.fori_loop(0, out.shape[0], clear, 0)

    def add(g, carry):
        for q in range(NV):
            base = jnp.where(me_p < (offs[4 * g + q, 0] >> 5), 4, 0)
            local, held = jnp.int32(0), jnp.int32(0)
            for j in range(4):
                slot = slots[foot[4 * g + q, base + j]]
                local = jnp.where((slot >> 6) == me_e, slot & 63, local)
                held = jnp.where((slot >> 6) == me_e, 1, held)

            @pl.when(held == 1)
            def _():
                out[local] = out[local] + pieces[g, q].astype(F32)
        return carry

    lax.fori_loop(0, NE, add, 0)


def total(footprints, offsets, tile_slot, pieces, shape):
    smem = pl.BlockSpec(memory_space=pltpu.SMEM)
    vmem = pl.BlockSpec(memory_space=pltpu.VMEM)
    return pl.pallas_call(
        total_kernel,
        out_shape=jax.ShapeDtypeStruct(shape, F32),
        in_specs=[smem, smem, smem, vmem],
        out_specs=vmem,
        compiler_params=pltpu.CompilerParams(vmem_limit_bytes=40 * 2**20),
        name="total",
    )(footprints, offsets, tile_slot, pieces)


def local(sky, kernels, coefs, observed, inv_var, footprints, offsets, tile_slot):
    fwd, adj = tables(kernels)
    pieces = fused(footprints, offsets, tile_slot, sky, coefs, observed, inv_var, fwd, adj)
    return total(footprints, offsets, tile_slot, pieces, sky.shape)


def solution(mesh):
    return jax.shard_map(
        local,
        mesh=mesh,
        in_specs=(
            P("exp", "pix", None),
            P(),
            P("exp", None, "pix", None),
            P("exp", "pix", None),
            P("exp", "pix", None),
            P(),
            P(),
            P(),
        ),
        out_specs=P("exp", "pix", None),
        check_vma=False,
    )
```

time: 203 us -> 87.8 us (0.43)
  waiting for transfers between devices: 81.9 us -> 0 us
  Pallas kernels: 18 us -> 82.1 us
  starting transfers between devices: 42.6 us -> 0 us
  local copies, waits for them, and re-layouts: 33.7 us -> 5.25 us
  other arithmetic: 22.7 us -> 0.09 us
  matrix products: 2.34 us -> 0 us
    all_to_all x4 -> x0, waiting for transfers between devices: 76.1 us -> none  [the longest x1 24.6 us: local(): lax.all_to_all(forward_rows, 'pix', split_axis=0, concat_axis=0, tiled=True)]
    pallas_call x1 -> x3, Pallas kernels: 18 us -> 82.1 us  [the longest x1 76.6 us: fused(): pl.pallas_call(fused_kernel, out_shape=jax.ShapeDtypeStruct((NE, NV, ROWS...]
    all_to_all x4 -> x0, starting transfers between devices: 33.2 us -> none  [the longest x1 9.89 us: local(): lax.all_to_all(to_owners, 'exp', split_axis=0, concat_axis=0, tiled=True)]
    gather x17 -> x0, local copies, waits for them, and re-layouts: 14.8 us -> none  [the longest x1 2.17 us: local(): mine = landed[(my_phase + strip_index) % strip_count]]
    select_n x16 -> x0, other arithmetic: 9.68 us -> none  [the longest x1 3.12 us: local(): jnp.where(back_has[:, None, None, None], pieces[back_visit], nothing)]
    ppermute x4 -> x0, starting transfers between devices: 9.47 us -> none  [the longest x2 5.29 us: passed_along(): return lax.ppermute(x, axis, pairs)]
    scatter-add x1 -> x0, other arithmetic: 6.95 us -> none  [local(): gradient.at[held_rows.reshape(-1)]]
    reshape x5 -> x0, local copies, waits for them, and re-layouts: 6.15 us -> none  [the longest x2 3.08 us: tables(): t.reshape(nb, 5, 5, tall, rows).transpose(1, 3, 2, 0, 4)]
  transfers between devices with their start and end apart: 8 -> 0, of which waited for: 6 -> 0; matrix products, arithmetic and copies ran while one was open for 8% -> 0% of each run, Pallas kernels for 0% -> 0%
where the time goes in v3:
time: 87.8 us; the launch traced here: 87.5 us
  Pallas kernels  82.1 us (94%)
  local copies, waits for them, and re-layouts  5.25 us (6%)
    pallas_call x1, Pallas kernels, fused(): pl.pallas_call(fused_kernel, out_shape=jax.ShapeDtypeStruct((NE, NV, ROWS...  76.6 us
    unnamed x9, local copies, waits for them, and re-layouts  5.25 us
    pallas_call x1, Pallas kernels, total(): pl.pallas_call(total_kernel, out_shape=jax.ShapeDtypeStruct(shape, F32),...  4.47 us

profile of v3, /device:TPU:1, one launch (start us, length us, event | category | flops | bytes accessed | tf_op | source)
XLA Modules:
  0.0 87.5 jit_solution(15215306400581412357)
XLA Ops:
  0.0 0.8 copy.12.foot
  0.8 0.8 copy.13.offs
  1.5 0.9 %copy.9 = bf16[6,25,25]{1,2,0:T(8,128)(2,1)S(1)} copy(bf16[6,25,25]{2,1,0:T(8,128)(2,1)} %param.9) | data formatting | bytes 15000 | tf_op args[1]
  2.5 0.1 pad_convert_fusion.kt
  2.5 1.0 %tables.1 = (bf16[192,1600]{1,0:T(8,128)(2,1)S(1)}, bf16[320,960]{1,0:T(8,128)(2,1)S(1)}) custom-call(f32[6,25,128]{2,1,0:T(8,128)S(1)} %pad_convert_fusion.kt), custom_call_target="tpu_custom_call" | custom-call | tf_op jit(solution)/shard_map/tables/pallas_call | solution.py:53
  3.6 0.0 copy-start
  3.6 1.1 %copy-done = f32[4,32,1536]{2,1,0:T(8,128)S(1)} copy-done((f32[4,32,1536]{2,1,0:T(8,128)S(1)}, f32[4,32,1536]{2,1,0:T(8,128)}, u32[]{:S(2)}) %copy-start) | copy-done | bytes 786456
  4.7 0.0 copy-start.1
  4.7 1.0 %copy-done.1 = bf16[4,32,1536]{2,1,0:T(8,128)(2,1)S(1)} copy-done((bf16[4,32,1536]{2,1,0:T(8,128)(2,1)S(1)}, bf16[4,32,1536]{2,1,0:T(8,128)(2,1)}, u32[]{:S(2)}) %copy-start.1) | copy-done | bytes 393240
  5.7 0.0 copy-start.2
  5.7 0.7 copy-done.2
  6.4 76.6 %fused.1.pieces = bf16[8,4,32,512]{3,2,1,0:T(8,128)(2,1)S(1)} custom-call(s32[32,8]{1,0:T(8,128)S(1)} %copy.12.foot, s32[32,2]{1,0:T(8,128)S(1)} %copy.13.offs, s32[512]{0:T(512)S(1)} %copy-done.2, bf16[64,32,512]{2,1,0:T(8,128)(2,1)} %sky_hbm.1, bf16[4,6,32,1536]{3,2,1,0:T(8,128)(2,1)} %coefs_hbm.1, f32[4,32,1536]{2,1,0:T(8,128)S(1)} %copy-done, ...), custom_call_target="tpu_custom_call" | custom-call | tf_op jit(solution)/shard_map/fused/pallas_call | solution.py:246
  83.0 4.5 %total.1 = f32[64,32,512]{2,1,0:T(8,128)} custom-call(s32[32,8]{1,0:T(8,128)S(1)} %copy.12.foot, s32[32,2]{1,0:T(8,128)S(1)} %copy.13.offs, s32[512]{0:T(512)S(1)} %copy-done.2, bf16[8,4,32,512]{3,2,1,0:T(8,128)(2,1)S(1)} %fused.1.pieces), custom_call_target="tpu_custom_call" | custom-call | tf_op jit(solution)/shard_map/total/pallas_call | solution.py:302
Async XLA Ops:
  3.6 1.1 %copy-start = (f32[4,32,1536]{2,1,0:T(8,128)S(1)}, f32[4,32,1536]{2,1,0:T(8,128)}, u32[]{:S(2)}) copy-start(f32[4,32,1536]{2,1,0:T(8,128)} %obs_hbm.1) | copy-start | bytes 2359300
  4.7 1.0 %copy-start.1 = (bf16[4,32,1536]{2,1,0:T(8,128)(2,1)S(1)}, bf16[4,32,1536]{2,1,0:T(8,128)(2,1)}, u32[]{:S(2)}) copy-start(bf16[4,32,1536]{2,1,0:T(8,128)(2,1)} %inv_hbm.1) | copy-start | bytes 1179652
  5.7 0.7 copy-start.2

commit v4 on v3

v4 whole, which is shorter than its diff:
```python
import jax
import jax.numpy as jnp
from jax import lax
from jax.experimental import pallas as pl
from jax.experimental.pallas import tpu as pltpu
from jax.sharding import PartitionSpec as P

E_AXIS, P_AXIS = "exp", "pix"
MESH_ID = pl.DeviceIdType.MESH
KS, NB, RIM, NV = 25, 6, 12, 4
NE, NP = 8, 16
ROWS, TALL, LANES = 32, 64, 128
WIDTH, SPAN, FULL, NCH = 1536, 1664, 2048, 13
BF, F32 = jnp.bfloat16, jnp.float32


def build_tables(kernels, kt, fwd, adj):
    lane = lax.broadcasted_iota(jnp.int32, (ROWS, LANES), 1)
    for b in range(NB):
        square = jnp.concatenate([kernels[b].astype(F32), jnp.zeros((KS, LANES - KS), F32)], axis=1)
        square = jnp.concatenate([square, jnp.zeros((LANES - KS, LANES), F32)], axis=0)
        kt[b] = pltpu.roll(square.T[0:ROWS], 4, axis=1)
    tail = {}
    for m in range(13):
        blocks = []
        for b in range(NB):
            low = pltpu.roll(jnp.broadcast_to(kt[b, 2 * m:2 * m + 1, :], (ROWS, LANES)), 0, axis=1, stride=1, stride_axis=0)
            if 2 * m + 1 < KS:
                high = pltpu.roll(
                    jnp.broadcast_to(kt[b, 2 * m + 1:2 * m + 2, :], (ROWS, LANES)), TALL, axis=1, stride=1, stride_axis=0
                )
                block = jnp.where(lane < TALL, low, high)
                fwd[b * ROWS:(b + 1) * ROWS, m * LANES:(m + 1) * LANES] = block.astype(BF)
            else:
                block = low
                fwd[b * ROWS:(b + 1) * ROWS, m * LANES:m * LANES + TALL] = block[:, :TALL].astype(BF)
            blocks.append(block)
        turned_a = jnp.concatenate(blocks[:4], axis=0).T
        turned_b = jnp.concatenate(blocks[4:] + [jnp.zeros((2 * ROWS, LANES), F32)], axis=0).T
        for h in range(2):
            v = 2 * m + h
            if v < KS:
                a, c = divmod(v, 5)
                adj[a * TALL:(a + 1) * TALL, c * LANES:(c + 1) * LANES] = turned_a[h * TALL:(h + 1) * TALL].astype(BF)
                tail[a, c] = turned_b[h * TALL:(h + 1) * TALL]
    wide_lane = lax.broadcasted_iota(jnp.int32, (TALL, LANES), 1)
    for a in range(5):
        for c in (0, 2):
            pair = jnp.where(wide_lane < 64, tail[a, c], pltpu.roll(tail[a, c + 1], 64, axis=1))
            adj[a * TALL:(a + 1) * TALL, 640 + c * 64:640 + c * 64 + LANES] = pair.astype(BF)
        adj[a * TALL:(a + 1) * TALL, 896:960] = tail[a, 4][:, :64].astype(BF)


def chunk_of(device, turn):
    return lax.rem(device + 2 * NP - turn, NP)


def forward_step(q, band, coef_ref, obs_ref, inv_ref, fwd, stack, wide):
    win = jnp.concatenate([band[c, q] for c in range(NCH)], axis=1)
    for v in range(KS):
        stack[v * TALL:(v + 1) * TALL, :] = win[:, v:v + WIDTH]
    nc = 512
    wide[0:128, WIDTH:] = jnp.zeros((128, SPAN - WIDTH), BF)
    wide[640:704, WIDTH:] = jnp.zeros((64, SPAN - WIDTH), BF)

    def chunk(n, carry):
        cols = pl.ds(pl.multiple_of(n * nc, nc), nc)
        blurred = jnp.dot(fwd[...], stack[:, cols], preferred_element_type=F32)
        coef = [coef_ref[q, b, :, cols].astype(F32) for b in range(NB)]
        model = coef[0] * blurred[0:ROWS]
        for b in range(1, NB):
            model = model + coef[b] * blurred[b * ROWS:(b + 1) * ROWS]
        resid = inv_ref[q, :, cols].astype(F32) * (model - obs_ref[q, :, cols])
        for b in range(NB):
            at = b * ROWS if b < 4 else 640 + (b - 4) * ROWS
            wide[at:at + ROWS, cols] = (coef[b] * resid).astype(BF)
        return carry

    lax.fori_loop(0, WIDTH // nc, chunk, 0)


def adjoint_step(q, adj, wide, back_ref):
    head, rest = wide[0:128, :], wide[640:704, :]
    for c in range(1, 5):
        wide[c * 128:(c + 1) * 128, :] = jnp.concatenate([jnp.zeros((128, c), BF), head[:, :SPAN - c]], axis=1)
        wide[640 + c * 64:640 + (c + 1) * 64, :] = jnp.concatenate([jnp.zeros((64, c), BF), rest[:, :SPAN - c]], axis=1)
    part = jnp.dot(adj[...], wide[...], preferred_element_type=F32)
    back = part[0:TALL]
    for a in range(1, 5):
        back = back + pltpu.roll(part[a * TALL:(a + 1) * TALL], 5 * a, axis=1)
    for c in range(NCH):
        back_ref[c, q] = back[:, c * LANES:(c + 1) * LANES].astype(BF)


SINGLE = ((0,), (1,), (2,), (3,))
GROUPS = {1: SINGLE, 2: SINGLE, 3: SINGLE, 4: SINGLE, 5: SINGLE, 6: SINGLE, 7: SINGLE}
TURNS = (0, 4, 8, 12)
ORDER = (
    (1, 0), (1, 1), (1, 2), (1, 3), (2, 0), (2, 1), (3, 0), (2, 2), (3, 1), (2, 3), (3, 2), (4, 0), (5, 0), (3, 3), (4, 1), (5, 1),
    (6, 0), (4, 2), (5, 2), (6, 1), (7, 0), (4, 3), (5, 3), (6, 2), (7, 1), (6, 3), (7, 2), (7, 3),
)


def group_of(step, q):
    for n, group in enumerate(GROUPS[step]):
        if q in group:
            return n, group.index(q)


def fused_kernel(foot_hbm, offs_hbm, slots_hbm, kernels, sky_hbm, coefs_hbm, obs_hbm, inv_hbm, pieces, target, *scratch):
    scratch = list(scratch)
    take = lambda count: [scratch.pop(0) for _ in range(count)]
    recv1, recv2, recv4 = take(len(GROUPS[1])), take(len(GROUPS[2])), take(len(GROUPS[5]))
    recv5, tiles = take(len(GROUPS[6])), take(NV)
    (foot, offs, slots, kt, fwd, adj, sky, coef, obs, inv, stage1, stage2, stage3, stage5, stage6, band, back, stack, wide,
     s1, r1, s2, r2, s3, r3, s4, r4, s5, r5, s6, r6, loads) = scratch
    me_e, me_p = lax.axis_index(E_AXIS), lax.axis_index(P_AXIS)
    first_loads = [
        pltpu.make_async_copy(src, dst, loads.at[k])
        for k, (src, dst) in enumerate(((foot_hbm, foot), (offs_hbm, offs), (slots_hbm, slots), (sky_hbm, sky)), 3)
    ]
    rest_loads = [
        pltpu.make_async_copy(src, dst, loads.at[k])
        for k, (src, dst) in enumerate(((coefs_hbm, coef), (obs_hbm, obs), (inv_hbm, inv)))
    ]
    for load in first_loads:
        load.start()
    barrier = pltpu.get_barrier_semaphore()
    for d in range(1, NE):
        pl.semaphore_signal(barrier, inc=1, device_id=(lax.rem(me_e + d, NE), me_p), device_id_type=MESH_ID)
    for d in range(1, NP):
        pl.semaphore_signal(barrier, inc=1, device_id=(me_e, lax.rem(me_p + d, NP)), device_id_type=MESH_ID)
    for load in first_loads:
        load.wait()
    for load in rest_loads:
        load.start()

    def fill(g, carry):
        for q in range(NV):
            base = jnp.where(me_p < (offs[0, 4 * g + q] >> 5), 4, 0)
            local, found = jnp.int32(0), jnp.int32(-1)
            for j in range(4):
                slot = slots[foot[base + j, 4 * g + q]]
                local = jnp.where((slot >> 6) == me_e, slot & 63, local)
                found = jnp.where((slot >> 6) == me_e, slot & 63, found)
            stage1[g, q] = sky[local]
            target[4 * g + q] = found
        return carry

    lax.fori_loop(0, NE, fill, 0)
    phase = [offs[0, 4 * me_e + q] >> 5 for q in range(NV)]
    shift = [offs[1, 4 * me_e + q] - RIM for q in range(NV)]
    source = []
    for q in range(NV):
        base = jnp.where(me_p < phase[q], 4, 0)
        source.append([slots[foot[base + j, 4 * me_e + q]] >> 6 for j in range(4)])
    pl.semaphore_wait(barrier, NE + NP - 2)

    sent = []

    def guarded(condition, action):
        if condition is None:
            action()
        else:
            pl.when(condition)(action)

    def exchange(count, me, device, src, dst, send, recv, sends=None, receives=None):
        inward = []
        for d in range(1, count):
            to, of = lax.rem(me + d, count), lax.rem(me + count - d, count)

            def make(slot, to=to):
                return pltpu.make_async_remote_copy(
                    src_ref=src(to), dst_ref=dst(slot), send_sem=send.at[to], recv_sem=recv.at[slot],
                    device_id=device(to), device_id_type=MESH_ID)

            go = None if sends is None else sends(to)
            come = None if receives is None else receives(of)
            guarded(go, lambda make=make: make(me).start())
            sent.append((go, lambda make=make: make(me).wait_send()))
            inward.append((come, lambda make=make, of=of: make(of).wait_recv()))
        return inward

    over_e, over_p = (lambda to: (to, me_p)), (lambda to: (me_e, to))

    def arrive(copies):
        for condition, action in copies:
            guarded(condition, action)

    def turn_of(group):
        return TURNS[group[0]]

    def chunk_at(device, turn):
        return jnp.minimum(chunk_of(device, turn), NCH - 1)

    def holds(turn):
        return lambda device: chunk_of(device, turn) < NCH

    def mine(turn):
        return lambda device: chunk_of(me_p, turn) < NCH

    def span(group):
        return pl.ds(group[0], len(group))

    def step1(n, group):
        qs = span(group)
        recv1[n][me_e] = stage1[me_e, group[0]:group[0] + len(group)]
        return exchange(NE, me_e, over_e, lambda to: stage1.at[to, qs], lambda i: recv1[n].at[i], s1.at[n], r1.at[n])

    def step2(n, group):
        qs, turn = span(group), turn_of(group)
        for q in group:
            m, k = group_of(1, q)
            row = jnp.concatenate([recv1[m][source[q][j], k] for j in range(4)], axis=1).astype(F32)
            row = pltpu.roll(row, (FULL - shift[q]) & (FULL - 1), axis=1)[:, :SPAN].astype(BF)
            for c in range(NCH):
                stage2[c, q] = row[:, c * LANES:(c + 1) * LANES]

        @pl.when(mine(turn)(me_p))
        def _():
            recv2[n][me_p] = stage2[chunk_at(me_p, turn), group[0]:group[0] + len(group)]

        return exchange(
            NP, me_p, over_p, lambda to: stage2.at[chunk_at(to, turn), qs], lambda i: recv2[n].at[i], s2.at[n], r2.at[n],
            holds(turn), mine(turn))

    def step3(n, group):
        qs, turn = span(group), turn_of(group)

        @pl.when(mine(turn)(me_p))
        def _():
            for q in group:
                m, k = group_of(2, q)
                for to in range(NP):
                    strip = (phase[q] + to) & 15
                    stage3[to, q, 16:48] = recv2[m][strip, k]
                    if to > 0:
                        stage3[to, q, 0:16] = recv2[m][(strip + 15) & 15, k, 16:32]
                    else:
                        stage3[to, q, 0:16] = jnp.zeros((16, LANES), BF)
                    if to < NP - 1:
                        stage3[to, q, 48:64] = recv2[m][(strip + 1) & 15, k, 0:16]
                    else:
                        stage3[to, q, 48:64] = jnp.zeros((16, LANES), BF)
                band[chunk_at(me_p, turn), q] = stage3[me_p, q]

        return exchange(
            NP, me_p, over_p, lambda to: stage3.at[to, qs], lambda i: band.at[chunk_at(i, turn), qs], s3.at[n],
            r3.at[n], mine(turn), holds(turn))

    def step4(n, group):
        for q in group:
            forward_step(q, band, coef, obs, inv, fwd, stack, wide)

    def step5(n, group):
        qs, turn = span(group), turn_of(group)
        for q in group:
            adjoint_step(q, adj, wide, back)

        @pl.when(mine(turn)(me_p))
        def _():
            recv4[n][me_p] = back[chunk_at(me_p, turn), group[0]:group[0] + len(group)]

        return exchange(
            NP, me_p, over_p, lambda to: back.at[chunk_at(to, turn), qs], lambda i: recv4[n].at[i], s4.at[n],
            r4.at[n], holds(turn), mine(turn))

    def step6(n, group):
        qs, turn = span(group), turn_of(group)

        def sums():
            for q in group:
                m, k = group_of(5, q)
                for to in range(NP):
                    strip = (to - phase[q]) & 15
                    centre = recv4[m][strip, k, 16:48].astype(F32)
                    above = jnp.where(strip > 0, recv4[m][(strip + 15) & 15, k, 48:64].astype(F32), 0.0)
                    below = jnp.where(strip < NP - 1, recv4[m][(strip + 1) & 15, k, 0:16].astype(F32), 0.0)
                    stage5[to, q, 0:16] = (centre[0:16] + above).astype(BF)
                    stage5[to, q, 16:32] = (centre[16:32] + below).astype(BF)
                recv5[n][chunk_at(me_p, turn), group.index(q)] = stage5[me_p, q]

        pl.when(mine(turn)(me_p))(sums)
        return exchange(
            NP, me_p, over_p, lambda to: stage5.at[to, qs], lambda i: recv5[n].at[chunk_at(i, turn)], s5.at[n],
            r5.at[n], mine(turn), holds(turn))

    def step7(n, group):
        qs = span(group)
        for q in group:
            m, k = group_of(6, q)
            parts = [recv5[m][c, k].astype(F32) for c in range(NCH)]
            row = jnp.concatenate(parts + [jnp.zeros((ROWS, FULL - SPAN), F32)], axis=1)
            row = pltpu.roll(row, shift[q], axis=1).astype(BF)
            for j in range(4):
                tiles[q][j] = row[:, j * 512:(j + 1) * 512]
            for o in range(NE):
                which = jnp.int32(0)
                for j in range(1, 4):
                    which = jnp.where(source[q][j] == o, j, which)
                stage6[o, q] = tiles[q][which]
            pieces[me_e, q] = stage6[me_e, q]
        return exchange(NE, me_e, over_e, lambda to: stage6.at[to, qs], lambda i: pieces.at[i, qs], s6.at[n], r6.at[n])

    steps = (step1, step2, step3, step4, step5, step6, step7)
    waiting = {}
    for n, g in ORDER:
        if (n, g) == (2, 0):
            build_tables(kernels, kt, fwd, adj)
        if (n, g) == (4, 0):
            for load in rest_loads:
                load.wait()
        group = GROUPS[n][g]
        for q in group:
            before = (n - 1, group_of(n - 1, q)[0]) if n > 1 else None
            if before in waiting:
                arrive(waiting.pop(before))
        copies = steps[n - 1](g, group)
        if copies is not None:
            waiting[n, g] = copies
    for key in sorted(waiting):
        arrive(waiting[key])
    arrive(sent)


def fused(footprints, offsets, tile_slot, kernels, sky, coefs, observed, inv_var):
    dma = pltpu.SemaphoreType.DMA
    smem = pl.BlockSpec(memory_space=pltpu.SMEM)
    vmem = pl.BlockSpec(memory_space=pltpu.VMEM)
    hbm = pl.BlockSpec(memory_space=pl.ANY)
    size = lambda n: [len(group) for group in GROUPS[n]]
    shapes = [(NE, k, ROWS, 512) for k in size(1)] + [(NP, k, ROWS, LANES) for k in size(2)]
    shapes += [(NP, k, TALL, LANES) for k in size(5)] + [(NCH, k, ROWS, LANES) for k in size(6)] + [(4, ROWS, 512)] * NV
    return pl.pallas_call(
        fused_kernel,
        out_shape=(jax.ShapeDtypeStruct((NE, NV, ROWS, 512), BF), jax.ShapeDtypeStruct((NE * NV,), jnp.int32)),
        in_specs=[hbm, hbm, hbm, vmem, hbm, hbm, hbm, hbm],
        out_specs=(vmem, smem),
        scratch_shapes=[pltpu.VMEM(s, BF) for s in shapes]
        + [
            pltpu.SMEM(footprints.shape, jnp.int32),
            pltpu.SMEM(offsets.shape, jnp.int32),
            pltpu.SMEM(tile_slot.shape, jnp.int32),
            pltpu.VMEM((NB, ROWS, LANES), F32),
            pltpu.VMEM((NB * ROWS, KS * TALL), BF),
            pltpu.VMEM((5 * TALL, 5 * NB * ROWS), BF),
            pltpu.VMEM(sky.shape, BF),
            pltpu.VMEM(coefs.shape, BF),
            pltpu.VMEM(observed.shape, F32),
            pltpu.VMEM(inv_var.shape, BF),
            pltpu.VMEM((NE, NV, ROWS, 512), BF),
            pltpu.VMEM((NCH, NV, ROWS, LANES), BF),
            pltpu.VMEM((NP, NV, TALL, LANES), BF),
            pltpu.VMEM((NP, NV, ROWS, LANES), BF),
            pltpu.VMEM((NE, NV, ROWS, 512), BF),
            pltpu.VMEM((NCH, NV, TALL, LANES), BF),
            pltpu.VMEM((NCH, NV, TALL, LANES), BF),
            pltpu.VMEM((KS * TALL, WIDTH), BF),
            pltpu.VMEM((5 * NB * ROWS, SPAN), BF),
        ]
        + [dma((len(GROUPS[n]), NE if n in (1, 7) else NP)) for n in (1, 2, 3, 5, 6, 7) for _ in range(2)] + [dma((7,))],
        compiler_params=pltpu.CompilerParams(collective_id=0, has_side_effects=True, vmem_limit_bytes=VLIM),
        name="fused",
    )(footprints, offsets, tile_slot, kernels, sky, coefs, observed, inv_var)


VLIM = 60 * 2**20


def total_kernel(target, pieces, out):
    step = pl.program_id(0)
    out[...] = jnp.zeros(out.shape, F32)
    count = out.shape[0]

    def add(e, carry):
        at = target[e] - step * count

        @pl.when((at >= 0) & (at < count))
        def _():
            out[at] = out[at] + pieces[e].astype(F32)

        return carry

    lax.fori_loop(0, NE * NV, add, 0)


def total(target, pieces, shape):
    pieces = pieces.reshape(NE * NV, ROWS, 512)
    return pl.pallas_call(
        total_kernel,
        grid=(4,),
        out_shape=jax.ShapeDtypeStruct(shape, F32),
        in_specs=[pl.BlockSpec(memory_space=pltpu.SMEM), pl.BlockSpec(pieces.shape, lambda i: (0, 0, 0))],
        out_specs=pl.BlockSpec((shape[0] // 4,) + shape[1:], lambda i: (i, 0, 0)),
        compiler_params=pltpu.CompilerParams(vmem_limit_bytes=VLIM),
        name="total",
    )(target, pieces)


def local(sky, kernels, coefs, observed, inv_var, footprints, offsets, tile_slot):
    pieces, target = fused(footprints.T, offsets.T, tile_slot, kernels, sky, coefs, observed, inv_var)
    return total(target, pieces, sky.shape)


def solution(mesh):
    return jax.shard_map(
        local,
        mesh=mesh,
        in_specs=(
            P("exp", "pix", None),
            P(),
            P("exp", None, "pix", None),
            P("exp", "pix", None),
            P("exp", "pix", None),
            P(),
            P(),
            P(),
        ),
        out_specs=P("exp", "pix", None),
        check_vma=False,
    )
```

time: 87.8 us -> 78.8 us (0.90)
  local copies, waits for them, and re-layouts: 5.25 us -> 0 us
  Pallas kernels: 82.1 us -> 78.6 us
    unnamed x9 -> x0, local copies, waits for them, and re-layouts: 5.25 us -> none
    pallas_call x3 -> x2, Pallas kernels: 82.1 us -> 78.6 us  [the longest x1 73.6 us: fused(): pl.pallas_call(fused_kernel, out_shape=(jax.ShapeDtypeStruct((NE, NV, ROW...]
where the time goes in v4:
time: 78.8 us; the launch traced here: 78.6 us
  Pallas kernels  78.6 us (100%)
    pallas_call x1, Pallas kernels, fused(): pl.pallas_call(fused_kernel, out_shape=(jax.ShapeDtypeStruct((NE, NV, ROW...  73.6 us
    pallas_call x1, Pallas kernels, total(): pl.pallas_call(total_kernel, grid=(4,), out_shape=jax.ShapeDtypeStruct(sh...  4.95 us

profile of v4, /device:TPU:1, one launch (start us, length us, event | category | flops | bytes accessed | tf_op | source)
XLA Modules:
  0.0 78.6 jit_solution(6269269064086132549)
XLA Ops:
  0.0 73.6 %fused.1 = (bf16[8,4,32,512]{3,2,1,0:T(8,128)(2,1)}, s32[32]{0:T(128)}) custom-call(s32[8,32]{1,0:T(8,128)} %bitcast.4, s32[2,32]{1,0:T(2,128)} %bitcast.5, s32[512]{0:T(512)} %slots_hbm.1, bf16[6,25,25]{2,1,0:T(8,128)(2,1)} %kernels.1, bf16[64,32,512]{2,1,0:T(8,128)(2,1)} %sky_hbm.1, bf16[4,6,32,1536]{3,2,1,0:T(8,128)(2,1)} %coefs_hbm.1, ...), custom_call_target="tpu_custom_call" | custom-call | tf_op jit(solution)/shard_map/fused/pallas_call | solution.py:334
  73.6 5.0 %total.1 = f32[64,32,512]{2,1,0:T(8,128)} custom-call(s32[32]{0:T(128)} %get-tuple-element.7.target, bf16[32,32,512]{2,1,0:T(8,128)(2,1)} %bitcast.3), custom_call_target="tpu_custom_call" | custom-call | tf_op jit(solution)/shard_map/total/pallas_call | solution.py:389

commit v5 on v4

--- a/solution.py
+++ b/solution.py
@@ -95,6 +95,10 @@
 SINGLE = ((0,), (1,), (2,), (3,))
 GROUPS = {1: SINGLE, 2: SINGLE, 3: SINGLE, 4: SINGLE, 5: SINGLE, 6: SINGLE, 7: SINGLE}
 TURNS = (0, 4, 8, 12)
+HOPS_E = (4, 2, 6, 3, 5, 7, 1)
+HOPS_P = (
+    (1, 0), (0, 1), (3, 0), (0, 3), (1, 2), (2, 1), (3, 2), (2, 3), (2, 0), (0, 2), (1, 1), (3, 3), (1, 3), (3, 1), (2, 2),
+)
 ORDER = (
     (1, 0), (1, 1), (1, 2), (1, 3), (2, 0), (2, 1), (3, 0), (2, 2), (3, 1), (2, 3), (3, 2), (4, 0), (5, 0), (3, 3), (4, 1), (5, 1),
     (6, 0), (4, 2), (5, 2), (6, 1), (7, 0), (4, 3), (5, 3), (6, 2), (7, 1), (6, 3), (7, 2), (7, 3),
@@ -164,24 +168,31 @@
         else:
             pl.when(condition)(action)
 
-    def exchange(count, me, device, src, dst, send, recv, sends=None, receives=None):
-        inward = []
-        for d in range(1, count):
-            to, of = lax.rem(me + d, count), lax.rem(me + count - d, count)
-
-            def make(slot, to=to):
-                return pltpu.make_async_remote_copy(
-                    src_ref=src(to), dst_ref=dst(slot), send_sem=send.at[to], recv_sem=recv.at[slot],
-                    device_id=device(to), device_id_type=MESH_ID)
-
-            go = None if sends is None else sends(to)
-            come = None if receives is None else receives(of)
-            guarded(go, lambda make=make: make(me).start())
-            sent.append((go, lambda make=make: make(me).wait_send()))
-            inward.append((come, lambda make=make, of=of: make(of).wait_recv()))
-        return inward
-
-    over_e, over_p = (lambda to: (to, me_p)), (lambda to: (me_e, to))
+    def taken(view, sem, counts):
+        def wait(count):
+            pltpu.make_async_copy(view(count), view(count), sem).wait()
+
+        return [(condition, lambda count=count: wait(count)) for condition, count in counts]
+
+    def exchange(partners, src, dst, send, recv, outward, inward, sends=None):
+        for to, device in partners:
+            def start(to=to, device=device):
+                pltpu.make_async_remote_copy(
+                    src_ref=src(to), dst_ref=dst, send_sem=send, recv_sem=recv,
+                    device_id=device, device_id_type=MESH_ID).start()
+
+            guarded(None if sends is None else sends(to), start)
+        sent.extend(taken(outward[0], send, outward[1]))
+        return taken(inward[0], recv, inward[1])
+
+    column, row_at = me_p // 4, lax.rem(me_p, 4)
+    exp_partners, pix_partners = [], []
+    for d in HOPS_E:
+        to = lax.rem(me_e + d, NE)
+        exp_partners.append((to, (to, me_p)))
+    for dx, dy in HOPS_P:
+        to = lax.rem(column + dx, 4) * 4 + lax.rem(row_at + dy, 4)
+        pix_partners.append((to, (me_e, to)))
 
     def arrive(copies):
         for condition, action in copies:
@@ -199,13 +210,21 @@
     def mine(turn):
         return lambda device: chunk_of(me_p, turn) < NCH
 
+    def to_all(turn):
+        return [(mine(turn)(me_p), NP - 1)]
+
+    def to_holders(turn):
+        return [(mine(turn)(me_p), NCH - 1), (jnp.logical_not(mine(turn)(me_p)), NCH)]
+
     def span(group):
         return pl.ds(group[0], len(group))
 
     def step1(n, group):
         qs = span(group)
         recv1[n][me_e] = stage1[me_e, group[0]:group[0] + len(group)]
-        return exchange(NE, me_e, over_e, lambda to: stage1.at[to, qs], lambda i: recv1[n].at[i], s1.at[n], r1.at[n])
+        return exchange(
+            exp_partners, lambda to: stage1.at[to, qs], recv1[n].at[me_e], s1.at[n], r1.at[n],
+            (lambda k: stage1.at[pl.ds(0, k), qs], [(None, NE - 1)]), (lambda k: recv1[n].at[pl.ds(0, k)], [(None, NE - 1)]))
 
     def step2(n, group):
         qs, turn = span(group), turn_of(group)
@@ -221,8 +240,9 @@
             recv2[n][me_p] = stage2[chunk_at(me_p, turn), group[0]:group[0] + len(group)]
 
         return exchange(
-            NP, me_p, over_p, lambda to: stage2.at[chunk_at(to, turn), qs], lambda i: recv2[n].at[i], s2.at[n], r2.at[n],
-            holds(turn), mine(turn))
+            pix_partners, lambda to: stage2.at[chunk_at(to, turn), qs], recv2[n].at[me_p], s2.at[n], r2.at[n],
+            (lambda k: stage2.at[pl.ds(0, k), qs], to_holders(turn)), (lambda k: recv2[n].at[pl.ds(0, k)], to_all(turn)),
+            holds(turn))
 
     def step3(n, group):
         qs, turn = span(group), turn_of(group)
@@ -245,8 +265,9 @@
                 band[chunk_at(me_p, turn), q] = stage3[me_p, q]
 
         return exchange(
-            NP, me_p, over_p, lambda to: stage3.at[to, qs], lambda i: band.at[chunk_at(i, turn), qs], s3.at[n],
-            r3.at[n], mine(turn), holds(turn))
+            pix_partners, lambda to: stage3.at[to, qs], band.at[chunk_at(me_p, turn), qs], s3.at[n], r3.at[n],
+            (lambda k: stage3.at[pl.ds(0, k), qs], to_all(turn)), (lambda k: band.at[pl.ds(0, k), qs], to_holders(turn)),
+            mine(turn))
 
     def step4(n, group):
         for q in group:
@@ -262,8 +283,9 @@
             recv4[n][me_p] = back[chunk_at(me_p, turn), group[0]:group[0] + len(group)]
 
         return exchange(
-            NP, me_p, over_p, lambda to: back.at[chunk_at(to, turn), qs], lambda i: recv4[n].at[i], s4.at[n],
-            r4.at[n], holds(turn), mine(turn))
+            pix_partners, lambda to: back.at[chunk_at(to, turn), qs], recv4[n].at[me_p], s4.at[n], r4.at[n],
+            (lambda k: back.at[pl.ds(0, k), qs], to_holders(turn)), (lambda k: recv4[n].at[pl.ds(0, k)], to_all(turn)),
+            holds(turn))
 
     def step6(n, group):
         qs, turn = span(group), turn_of(group)
@@ -282,8 +304,9 @@
 
         pl.when(mine(turn)(me_p))(sums)
         return exchange(
-            NP, me_p, over_p, lambda to: stage5.at[to, qs], lambda i: recv5[n].at[chunk_at(i, turn)], s5.at[n],
-            r5.at[n], mine(turn), holds(turn))
+            pix_partners, lambda to: stage5.at[to, qs], recv5[n].at[chunk_at(me_p, turn)], s5.at[n], r5.at[n],
+            (lambda k: stage5.at[pl.ds(0, k), qs], to_all(turn)), (lambda k: recv5[n].at[pl.ds(0, k)], to_holders(turn)),
+            mine(turn))
 
     def step7(n, group):
         qs = span(group)
@@ -300,7 +323,9 @@
                     which = jnp.where(source[q][j] == o, j, which)
                 stage6[o, q] = tiles[q][which]
             pieces[me_e, q] = stage6[me_e, q]
-        return exchange(NE, me_e, over_e, lambda to: stage6.at[to, qs], lambda i: pieces.at[i, qs], s6.at[n], r6.at[n])
+        return exchange(
+            exp_partners, lambda to: stage6.at[to, qs], pieces.at[me_e, qs], s6.at[n], r6.at[n],
+            (lambda k: stage6.at[pl.ds(0, k), qs], [(None, NE - 1)]), (lambda k: pieces.at[pl.ds(0, k), qs], [(None, NE - 1)]))
 
     steps = (step1, step2, step3, step4, step5, step6, step7)
     waiting = {}
@@ -358,7 +383,7 @@
             pltpu.VMEM((KS * TALL, WIDTH), BF),
             pltpu.VMEM((5 * NB * ROWS, SPAN), BF),
         ]
-        + [dma((len(GROUPS[n]), NE if n in (1, 7) else NP)) for n in (1, 2, 3, 5, 6, 7) for _ in range(2)] + [dma((7,))],
+        + [dma((len(GROUPS[n]),)) for n in (1, 2, 3, 5, 6, 7) for _ in range(2)] + [dma((7,))],
         compiler_params=pltpu.CompilerParams(collective_id=0, has_side_effects=True, vmem_limit_bytes=VLIM),
         name="fused",
     )(footprints, offsets, tile_slot, kernels, sky, coefs, observed, inv_var)

time: 78.8 us -> 73.4 us (0.931)
  Pallas kernels: 78.6 us -> 73.2 us
    pallas_call x1, Pallas kernels: 73.6 us -> 68.2 us  [fused(): pl.pallas_call(fused_kernel, out_shape=(jax.ShapeDtypeStruct((NE, NV, ROW...]
where the time goes in v5:
time: 73.4 us; the launch traced here: 73.2 us
  Pallas kernels  73.2 us (100%)
    pallas_call x1, Pallas kernels, fused(): pl.pallas_call(fused_kernel, out_shape=(jax.ShapeDtypeStruct((NE, NV, ROW...  68.2 us
    pallas_call x1, Pallas kernels, total(): pl.pallas_call(total_kernel, grid=(4,), out_shape=jax.ShapeDtypeStruct(sh...  4.94 us

profile of v5, /device:TPU:1, one launch (start us, length us, event | category | flops | bytes accessed | tf_op | source)
XLA Modules:
  0.0 73.2 jit_solution(10411701502770284918)
XLA Ops:
  0.0 68.2 %fused.1 = (bf16[8,4,32,512]{3,2,1,0:T(8,128)(2,1)}, s32[32]{0:T(128)}) custom-call(s32[8,32]{1,0:T(8,128)} %bitcast.4, s32[2,32]{1,0:T(2,128)} %bitcast.5, s32[512]{0:T(512)} %slots_hbm.1, bf16[6,25,25]{2,1,0:T(8,128)(2,1)} %kernels.1, bf16[64,32,512]{2,1,0:T(8,128)(2,1)} %sky_hbm.1, bf16[4,6,32,1536]{3,2,1,0:T(8,128)(2,1)} %coefs_hbm.1, ...), custom_call_target="tpu_custom_call" | custom-call | tf_op jit(solution)/shard_map/fused/pallas_call | solution.py:359
  68.3 4.9 %total.1 = f32[64,32,512]{2,1,0:T(8,128)} custom-call(s32[32]{0:T(128)} %get-tuple-element.7.target, bf16[32,32,512]{2,1,0:T(8,128)(2,1)} %bitcast.3), custom_call_target="tpu_custom_call" | custom-call | tf_op jit(solution)/shard_map/total/pallas_call | solution.py:414

commit v6 on v5

--- a/solution.py
+++ b/solution.py
@@ -59,7 +59,7 @@
     win = jnp.concatenate([band[c, q] for c in range(NCH)], axis=1)
     for v in range(KS):
         stack[v * TALL:(v + 1) * TALL, :] = win[:, v:v + WIDTH]
-    nc = 512
+    nc = 1536
     wide[0:128, WIDTH:] = jnp.zeros((128, SPAN - WIDTH), BF)
     wide[640:704, WIDTH:] = jnp.zeros((64, SPAN - WIDTH), BF)
 
@@ -99,10 +99,7 @@
 HOPS_P = (
     (1, 0), (0, 1), (3, 0), (0, 3), (1, 2), (2, 1), (3, 2), (2, 3), (2, 0), (0, 2), (1, 1), (3, 3), (1, 3), (3, 1), (2, 2),
 )
-ORDER = (
-    (1, 0), (1, 1), (1, 2), (1, 3), (2, 0), (2, 1), (3, 0), (2, 2), (3, 1), (2, 3), (3, 2), (4, 0), (5, 0), (3, 3), (4, 1), (5, 1),
-    (6, 0), (4, 2), (5, 2), (6, 1), (7, 0), (4, 3), (5, 3), (6, 2), (7, 1), (6, 3), (7, 2), (7, 3),
-)
+ORDER = ((1, 0), (1, 1), (1, 2), (1, 3), (2, 0), (2, 1), (3, 0), (2, 2), (3, 1), (2, 3), (4, 0), (3, 2), (5, 0), (3, 3), (4, 1), (5, 1), (4, 2), (6, 0), (5, 2), (4, 3), (6, 1), (5, 3), (7, 0), (6, 2), (7, 1), (6, 3), (7, 2), (7, 3))
 
 
 def group_of(step, q):
@@ -413,10 +410,10 @@
     pieces = pieces.reshape(NE * NV, ROWS, 512)
     return pl.pallas_call(
         total_kernel,
-        grid=(4,),
+        grid=(2,),
         out_shape=jax.ShapeDtypeStruct(shape, F32),
         in_specs=[pl.BlockSpec(memory_space=pltpu.SMEM), pl.BlockSpec(pieces.shape, lambda i: (0, 0, 0))],
-        out_specs=pl.BlockSpec((shape[0] // 4,) + shape[1:], lambda i: (i, 0, 0)),
+        out_specs=pl.BlockSpec((shape[0] // 2,) + shape[1:], lambda i: (i, 0, 0)),
         compiler_params=pltpu.CompilerParams(vmem_limit_bytes=VLIM),
         name="total",
     )(target, pieces)

time: 73.4 us -> 67 us (0.913)
  Pallas kernels: 73.2 us -> 66.8 us
    pallas_call x1, Pallas kernels: 68.2 us -> 62.9 us  [fused(): pl.pallas_call(fused_kernel, out_shape=(jax.ShapeDtypeStruct((NE, NV, ROW...]
    pallas_call x1, Pallas kernels: 4.94 us -> 3.94 us  [total(): pl.pallas_call(total_kernel, grid=(2,), out_shape=jax.ShapeDtypeStruct(sh...]
where the time goes in v6:
time: 67 us; the launch traced here: 66.8 us
  Pallas kernels  66.8 us (100%)
    pallas_call x1, Pallas kernels, fused(): pl.pallas_call(fused_kernel, out_shape=(jax.ShapeDtypeStruct((NE, NV, ROW...  62.9 us
    pallas_call x1, Pallas kernels, total(): pl.pallas_call(total_kernel, grid=(2,), out_shape=jax.ShapeDtypeStruct(sh...  3.94 us

profile of v6, /device:TPU:1, one launch (start us, length us, event | category | flops | bytes accessed | tf_op | source)
XLA Modules:
  0.0 66.8 jit_solution(17186194354498833338)
XLA Ops:
  0.0 62.9 %fused.1 = (bf16[8,4,32,512]{3,2,1,0:T(8,128)(2,1)}, s32[32]{0:T(128)}) custom-call(s32[8,32]{1,0:T(8,128)} %bitcast.4, s32[2,32]{1,0:T(2,128)} %bitcast.5, s32[512]{0:T(512)} %slots_hbm.1, bf16[6,25,25]{2,1,0:T(8,128)(2,1)} %kernels.1, bf16[64,32,512]{2,1,0:T(8,128)(2,1)} %sky_hbm.1, bf16[4,6,32,1536]{3,2,1,0:T(8,128)(2,1)} %coefs_hbm.1, ...), custom_call_target="tpu_custom_call" | custom-call | tf_op jit(solution)/shard_map/fused/pallas_call | solution.py:356
  62.9 3.9 %total.1 = f32[64,32,512]{2,1,0:T(8,128)} custom-call(s32[32]{0:T(128)} %get-tuple-element.7.target, bf16[32,32,512]{2,1,0:T(8,128)(2,1)} %bitcast.3), custom_call_target="tpu_custom_call" | custom-call | tf_op jit(solution)/shard_map/total/pallas_call | solution.py:411
